TPU v7x, 1024 devices: a whole 4x4x32 slice. The times are simulated.
1024 devices in a mesh: node: 32 (over z), local: 32 (over x, y, core).
Axes of the slice: x: 4, y: 4, z: 32, core: 2. Of those that a mesh axis runs over, the one named last changes fastest.
Arguments:
- out_grad: bfloat16 [512, 7168], P('node', 'local'), may hold values from -6 to 6
- groups: int32 [512, 4], P('node'), may hold values from 0 to 31, as said below
- route_weight: float32 [512, 4], P('node'), may hold values from 0.05 to 0.6
- saved_input: bfloat16 [4096, 7168], P('node'), may hold values from -6 to 6
- w_gate: bfloat16 [7168, 65536], P(None, ('node', 'local')), may hold values from -0.3125 to 0.3125
- w_up: bfloat16 [7168, 65536], P(None, ('node', 'local')), may hold values from -0.3125 to 0.3125
- w_down: bfloat16 [65536, 7168], P(('node', 'local')), may hold values from -0.0625 to 0.0625
Outputs:
- in_grad: bfloat16 [512, 7168], P('node', 'local')
- score_grad: float32 [512, 4], P('node')
Inputs may be any that keep to these rules, and one draw needn't show every extreme that they name: Each token names 4 different node groups. Of the tokens of one node group, at most 4 name any one node group; in every draw some node group is named by exactly 4 tokens of every node group.
All inputs are finite; a program needn't handle non-finite values.
Results may differ from a plain program's by a relative error of at most 0.022.
Values may be sent and summed in bfloat16 or wider, within the bound.
No kernel may reach another device: no remote copies, remote signals or barrier semaphores. Data moves between devices by JAX's collectives and lax.ppermute only.
A program may use at most 32 MiB of HBM per device.

v0:
```python
import jax
import jax.numpy as jnp
from jax import lax
from jax.sharding import PartitionSpec as P

FF = 2048
EXP_NODE = 1
GROUP_MOST = 4


HIGH = lax.Precision.HIGHEST


def visit_tables(groups, node_count, capacity):
    node_ids = jnp.arange(node_count, dtype=jnp.int32)
    chosen_int = (groups[:, :, None] == node_ids).astype(jnp.int32)
    visits = jnp.sum(chosen_int, axis=1)
    slot_rank = jnp.cumsum(visits, axis=0) - visits
    slot_ids = jnp.arange(capacity, dtype=jnp.int32)
    placement = visits[:, :, None] * (slot_rank[:, :, None] == slot_ids).astype(jnp.int32)
    return (chosen_int.astype(jnp.float32), placement.astype(jnp.float32))


def on_device(out_grad, groups, route_weight, saved_input, w_gate, w_up, w_down):
    tokens = out_grad.shape[0]
    node_count = lax.axis_size("node")
    capacity = tokens * min(node_count, 8) // node_count
    row_count = node_count * capacity
    chosen, placement = visit_tables(groups, node_count, capacity)
    flat_place = placement.reshape(tokens, row_count)
    rounded_scale = lax.optimization_barrier(route_weight.astype(jnp.bfloat16))
    route_scale = rounded_scale.astype(jnp.float32).reshape(tokens, GROUP_MOST, EXP_NODE)
    node_scale = jnp.einsum("tij,tie->tje", chosen, route_scale, precision=HIGH)
    send_grad = lax.dot_general(
        flat_place.astype(jnp.bfloat16),
        out_grad,
        (((0,), (0,)), ((), ())),
        preferred_element_type=jnp.float32,
    )
    send_grad = send_grad.astype(jnp.bfloat16).reshape(node_count, capacity, -1)
    send_scale = jnp.einsum("tjc,tje->jce", placement, node_scale, precision=HIGH).astype(
        jnp.bfloat16
    )
    recv_grad, recv_scale = (
        lax.all_to_all(send_grad, "node", split_axis=0, concat_axis=0, tiled=True),
        lax.all_to_all(send_scale, "node", split_axis=0, concat_axis=0, tiled=True),
    )
    slice_grad = recv_grad.reshape(row_count, -1)
    arriving_scale = recv_scale.reshape(row_count, EXP_NODE).astype(jnp.float32)
    width_dev = w_gate.shape[1]
    expert_here = lax.axis_index("local") * width_dev // FF
    expert_pick = (jnp.arange(EXP_NODE, dtype=jnp.int32) == expert_here).astype(jnp.float32)
    row_scale = jnp.sum(arriving_scale * expert_pick, axis=1, keepdims=True)
    gate_pre = jnp.dot(saved_input, w_gate, preferred_element_type=jnp.float32)
    up_pre = jnp.dot(saved_input, w_up, preferred_element_type=jnp.float32)
    full_grad = lax.all_gather(slice_grad, "local", axis=1, tiled=True)
    down_grad = lax.dot_general(
        full_grad, w_down, (((1,), (1,)), ((), ())), preferred_element_type=jnp.float32
    )
    sigmoid_gate = jax.nn.sigmoid(gate_pre)
    silu_value = gate_pre * sigmoid_gate
    activation = silu_value * up_pre
    own_score = jnp.sum(activation * down_grad, axis=1, keepdims=True) * expert_pick
    hidden_grad = row_scale * down_grad
    gate_grad = (
        hidden_grad * up_pre * sigmoid_gate * (1.0 + gate_pre * (1.0 - sigmoid_gate))
    ).astype(jnp.bfloat16)
    up_grad = (hidden_grad * silu_value).astype(jnp.bfloat16)
    term = lax.dot_general(
        w_gate, gate_grad, (((1,), (1,)), ((), ())), preferred_element_type=jnp.float32
    )
    feature_part = lax.psum_scatter(
        (
            term
            + lax.dot_general(
                w_up, up_grad, (((1,), (1,)), ((), ())), preferred_element_type=jnp.float32
            )
        ).astype(jnp.bfloat16),
        "local",
        scatter_dimension=0,
        tiled=True,
    ).astype(jnp.float32)
    score_send = lax.psum(own_score, "local")
    score_payload = score_send.reshape(node_count, capacity, EXP_NODE).transpose(2, 0, 1)
    back_part, back_score = (
        lax.all_to_all(
            feature_part.reshape(-1, node_count, capacity).astype(jnp.bfloat16),
            "node",
            split_axis=1,
            concat_axis=1,
            tiled=True,
        ).astype(jnp.float32),
        lax.all_to_all(
            score_payload.astype(jnp.bfloat16), "node", split_axis=1, concat_axis=1, tiled=True
        ).astype(score_payload.dtype),
    )
    token_part = jnp.dot(back_part.reshape(-1, row_count), flat_place.T, precision=HIGH)
    in_grad = token_part.T.astype(jnp.bfloat16)
    values = jnp.einsum("tjc,ejc->tje", placement, back_score, precision=HIGH)
    score_grad = jnp.einsum("tij,tje->tie", chosen, values, precision=HIGH).reshape(tokens, -1)
    return (in_grad, score_grad)


def solution(mesh):
    placed = (
        P("node", "local"),
        P("node", None),
        P("node", None),
        P("node", None),
        P(None, ("node", "local")),
        P(None, ("node", "local")),
        P(("node", "local"), None),
    )
    return jax.shard_map(
        on_device,
        mesh=mesh,
        in_specs=placed,
        out_specs=(P("node", "local"), P("node", None)),
        check_vma=False,
    )
```

profile of v0, /device:TPU:24, one launch (start us, length us, event | category | flops | bytes accessed | tf_op | source)
XLA Modules:
  0.0 323.1 jit_solution(16424807714814817299)
XLA Ops:
  7.2 0.9 convert_reduce_fusion
  8.3 0.1 eq.51
  8.5 0.9 convolution_convert_fusion
  9.6 54.4 %all_to_all.20 = bf16[32,4,224]{2,1,0:T(4,128)(2,1)S(1)} all-to-all(bf16[32,4,224]{2,1,0:T(4,128)(2,1)S(1)} %reshape.92), channel_id=1, replica_groups=mesh['node'=32,'local'=32] {'node'}, dimensions={0} | all-to-all | bytes 114688 | tf_op jit(solution)/shard_map/all_to_all | solution.py:45
  64.1 0.7 copy.35
  64.8 0.7 convert_element_type.82
  65.6 0.8 convert_convert_fusion.1
  66.3 0.2 fusion.12
  66.6 0.1 multiply_reduce_fusion
  66.8 0.7 copy.33
  67.6 3.8 %all-to-all-start = ((bf16[32,4,1]{1,2,0:T(2,128)(2,1)}), bf16[32,4,1]{1,2,0:T(2,128)(2,1)S(1)}, u32[]{:S(2)}, u32[]{:S(2)}) async-start(bf16[32,4,1]{1,2,0:T(2,128)(2,1)} %copy.33), calls=%async_computation | async-start | bytes 32768 | tf_op jit(solution)/shard_map/all_to_all | solution.py:46
  71.5 1.9 fusion.24
  73.4 0.7 fusion.23
  74.2 19.5 %all-to-all-done = bf16[32,4,1]{1,2,0:T(2,128)(2,1)S(1)} async-done(((bf16[32,4,1]{1,2,0:T(2,128)(2,1)}), bf16[32,4,1]{1,2,0:T(2,128)(2,1)S(1)}, u32[]{:S(2)}, u32[]{:S(2)}) %all-to-all-start) | async-done | bytes 288 | tf_op jit(solution)/shard_map/all_to_all | solution.py:46
  93.9 31.0 %all-gather.2.cloned.1.call-done = bf16[128,7168]{0,1:T(8,128)(2,1)} async-done(((bf16[128,224]{0,1:T(8,128)(2,1)}), bf16[128,7168]{0,1:T(8,128)(2,1)}) %all-gather.2.cloned.1.call-update) | async-done | bytes 1835024 | tf_op jit(solution)/shard_map/all_gather | solution.py:56
  124.9 2.3 multiply_reduce_fusion.2
  127.2 0.7 fusion.14
  127.9 0.5 copy-done.3
  128.3 1.9 fusion.1
  130.2 3.9 %copy.55 = bf16[7168,128]{1,0:T(8,128)(2,1)} copy(bf16[7168,128]{0,1:T(8,128)(2,1)} %fusion.1) | data formatting | bytes 3670016
  134.2 50.8 %psum.7 = bf16[128,1]{0,1:T(2,128)(2,1)S(1)} all-reduce(f32[128,1]{0,1:T(1,128)S(1)} %multiply_bitcast_fusion), channel_id=1, replica_groups=mesh['node'=32,'local'=32] {'local'}, use_global_device_ids=true, to_apply=%region_4.5 | all-reduce | flops 128 | bytes 768 | tf_op jit(solution)/shard_map/psum | solution.py:83
  185.0 0.7 convert_element_type.98
  185.7 22.9 %all-to-all-start.3 = ((bf16[1,32,4]{2,0,1:T(2,128)(2,1)}), bf16[1,32,4]{2,0,1:T(2,128)(2,1)S(1)}, u32[]{:S(2)}, u32[]{:S(2)}) async-start(bf16[1,32,4]{2,0,1:T(2,128)(2,1)} %convert_element_type.98), calls=%async_computation.3 | async-start | bytes 32768 | tf_op jit(solution)/shard_map/all_to_all | solution.py:93
  208.7 58.0 %reduce-scatter.4.cloned.1.call-done = bf16[224,128]{1,0:T(8,128)(2,1)} async-done(((bf16[7168,128]{1,0:T(8,128)(2,1)}), bf16[224,128]{1,0:T(8,128)(2,1)}) %reduce-scatter.4.cloned.1.call-update) | async-done | bytes 57360
  266.7 0.9 copy.56
  267.6 0.6 convert_element_type.94
  268.2 22.6 %all-to-all-start.2 = ((bf16[224,32,4]{0,2,1:T(4,128)(2,1)}), bf16[224,32,4]{0,2,1:T(4,128)(2,1)S(1)}, u32[]{:S(2)}, u32[]{:S(2)}) async-start(bf16[224,32,4]{0,2,1:T(4,128)(2,1)} %convert_element_type.94), calls=%async_computation.2 | async-start | bytes 131072 | tf_op jit(solution)/shard_map/all_to_all | solution.py:86
  291.0 0.1 copy.49
  291.1 0.2 fusion.5
  291.4 0.7 multiply_reduce_fusion.1
  292.2 23.2 %all-to-all-done.2 = bf16[224,32,4]{0,2,1:T(4,128)(2,1)S(1)} async-done(((bf16[224,32,4]{0,2,1:T(4,128)(2,1)}), bf16[224,32,4]{0,2,1:T(4,128)(2,1)S(1)}, u32[]{:S(2)}, u32[]{:S(2)}) %all-to-all-start.2) | async-done | bytes 57376 | tf_op jit(solution)/shard_map/all_to_all | solution.py:86
  315.4 0.8 fusion.2
  (34 shorter events, 1.2 us)
Async XLA Ops:
  7.2 64.3 %copy-start = (bf16[128,7168]{1,0:T(8,128)(2,1)S(1)}, bf16[128,7168]{1,0:T(8,128)(2,1)}, u32[]{:S(2)}) copy-start(bf16[128,7168]{1,0:T(8,128)(2,1)} %param.10) | copy-start | bytes 5505028
  7.2 117.7 %all-gather.2.cloned.1.call-start = ((), (), s32[]{:S(2)}) async-start(), calls=%async_computation.5 | async-start | bytes 1892352 | tf_op jit(solution)/shard_map/all_gather | solution.py:56
  9.5 63.9 %copy-start.2 = (bf16[7168,64]{0,1:T(8,128)(2,1)S(1)}, bf16[7168,64]{0,1:T(8,128)(2,1)}, u32[]{:S(2)}) copy-start(bf16[7168,64]{0,1:T(8,128)(2,1)} %param.12) | copy-start | bytes 2752516
  67.6 26.2 %all-to-all-start = ((bf16[32,4,1]{1,2,0:T(2,128)(2,1)}), bf16[32,4,1]{1,2,0:T(2,128)(2,1)S(1)}, u32[]{:S(2)}, u32[]{:S(2)}) async-start(bf16[32,4,1]{1,2,0:T(2,128)(2,1)} %copy.33), calls=%async_computation | async-start | bytes 32768 | tf_op jit(solution)/shard_map/all_to_all | solution.py:46
  71.4 195.3 %reduce-scatter.4.cloned.1.call-start = ((), (), s32[]{:S(2)}) async-start(), calls=%async_computation.6 | async-start | bytes 1892352
  74.2 53.0 %copy-start.1 = (bf16[7168,64]{0,1:T(8,128)(2,1)S(1)}, bf16[7168,64]{0,1:T(8,128)(2,1)}, u32[]{:S(2)}) copy-start(bf16[7168,64]{0,1:T(8,128)(2,1)} %param.11) | copy-start | bytes 2752516
  127.2 1.2 copy-start.3
  134.2 157.3 %copy-start.4 = (s32[16,4]{0,1:T(4,128)S(1)}, s32[16,4]{0,1:T(4,128)}, u32[]{:S(2)}) copy-start(s32[16,4]{0,1:T(4,128)} %param.8) | copy-start | bytes 772
  185.7 82.5 %all-to-all-start.3 = ((bf16[1,32,4]{2,0,1:T(2,128)(2,1)}), bf16[1,32,4]{2,0,1:T(2,128)(2,1)S(1)}, u32[]{:S(2)}, u32[]{:S(2)}) async-start(bf16[1,32,4]{2,0,1:T(2,128)(2,1)} %convert_element_type.98), calls=%async_computation.3 | async-start | bytes 32768 | tf_op jit(solution)/shard_map/all_to_all | solution.py:93
  268.2 47.2 %all-to-all-start.2 = ((bf16[224,32,4]{0,2,1:T(4,128)(2,1)}), bf16[224,32,4]{0,2,1:T(4,128)(2,1)S(1)}, u32[]{:S(2)}, u32[]{:S(2)}) async-start(bf16[224,32,4]{0,2,1:T(4,128)(2,1)} %convert_element_type.94), calls=%async_computation.2 | async-start | bytes 131072 | tf_op jit(solution)/shard_map/all_to_all | solution.py:86
Sparse Core Ops, SparseCore 0:
  64.9 59.9 all-gather.1
  134.3 132.3 reduce-scatter.3
where the time goes:
time: 324 us; the launch traced here: 323 us
  waiting for transfers between devices  132 us (41%)
  blocking collectives  105 us (32%)
  starting transfers between devices  49.5 us (15%)
  between operations  14.3 us (4%)
  matrix products  9.73 us (3%)
  local copies, waits for them, and re-layouts  9.24 us (3%)
  other arithmetic  3.33 us (1%)
    unnamed x3, waiting for transfers between devices  58 us
    all_to_all x1, blocking collectives, on_device(): lax.all_to_all(send_grad, 'node', split_axis=0, concat_axis=0, tiled=True)  54.4 us
    psum x1, blocking collectives, on_device(): score_send = lax.psum(own_score, 'local')  50.8 us
    all_gather x1, waiting for transfers between devices, on_device(): full_grad = lax.all_gather(slice_grad, 'local', axis=1, tiled=True)  31 us
    all_to_all x1, waiting for transfers between devices, on_device(): lax.all_to_all(feature_part.reshape(-1, node_count, capacity).astype(jnp....  23.2 us
    all_to_all x1, starting transfers between devices, on_device(): lax.all_to_all(score_payload.astype(jnp.bfloat16), 'node', split_axis=1,...  22.9 us
    all_to_all x1, starting transfers between devices, on_device(): lax.all_to_all(feature_part.reshape(-1, node_count, capacity).astype(jnp....  22.6 us
    all_to_all x1, waiting for transfers between devices, on_device(): lax.all_to_all(send_scale, 'node', split_axis=0, concat_axis=0, tiled=True)  19.5 us
  transfers between devices with their start and end apart: 5, of which 4 were waited for; matrix products, arithmetic and copies ran while one was open for 3% of the time, Pallas kernels for 0%

commit v1 on v0

v1 whole, which is shorter than its diff:
```python
import jax
import jax.numpy as jnp
from jax import lax
from jax.experimental import pallas as pl
from jax.experimental.pallas import tpu as pltpu
from jax.sharding import PartitionSpec as P

GROUP_MOST = 4
CAP = 4
LANES = 128
BF16 = jnp.bfloat16
F32 = jnp.float32
ROW_PAD = 240


def dot(a, b, contract):
    return lax.dot_general(
        a, b, ((contract[:1], contract[1:]), ((), ())), preferred_element_type=F32
    )


def iota(shape, dim):
    return lax.broadcasted_iota(jnp.int32, shape, dim)


def send_kernel(grad_ref, groups_ref, weight_ref, send_ref, place_ref):
    tokens, width = grad_ref.shape
    rows = send_ref.shape[0]
    row = iota((rows, tokens), 0)
    node, half, slot = row // (2 * CAP), row // CAP % 2, row % CAP
    named = [(groups_ref[i : i + 1, :] == node).astype(F32) for i in range(GROUP_MOST)]
    visits = named[0] + named[1] + named[2] + named[3]
    before = (iota((tokens, tokens), 0) < iota((tokens, tokens), 1)).astype(BF16)
    rank = dot(visits.astype(BF16), before, (1, 0))
    here = (rank == slot.astype(F32)).astype(F32)
    rounded = weight_ref[...].astype(BF16).astype(F32)
    scale = jnp.zeros((rows, tokens), F32)
    for i in range(GROUP_MOST):
        scale = scale + named[i] * rounded[i : i + 1, :]
    low = (half == 0).astype(F32) * here
    high = (half == 1).astype(F32) * here
    grad = grad_ref[...]
    rest = width - LANES
    grad_high = jnp.concatenate(
        [grad[:, LANES:].astype(F32), jnp.zeros((tokens, LANES - rest), F32)], axis=1
    ).astype(BF16)
    total = dot((low * visits).astype(BF16), grad[:, :LANES], (1, 0))
    total = total + dot((high * visits).astype(BF16), grad_high, (1, 0))
    row_scale = jnp.sum(high * scale, axis=1, keepdims=True)
    total = total + jnp.where(iota(total.shape, 1) == rest, row_scale, 0.0)
    send_ref[...] = total.astype(BF16)
    parts = [(part * named[i]) for part in (low, high) for i in range(GROUP_MOST)]
    place_ref[...] = jnp.concatenate(parts, axis=1).astype(BF16)


def pick(half, rows, arrivals):
    row, arrival = iota((rows, arrivals), 0), iota((rows, arrivals), 1)
    same = (row // (2 * CAP) == arrival // CAP) & (row % CAP == arrival % CAP)
    return (same & (row // CAP % 2 == half)).astype(BF16)


def spread_kernel(recv_ref, spread_ref, scale_ref):
    rows = recv_ref.shape[0]
    copies, width, arrivals = spread_ref.shape
    recv = recv_ref[...]
    low = dot(recv, pick(0, rows, arrivals), (0, 0))
    high = dot(recv, pick(1, rows, arrivals), (0, 0))
    rest = width - LANES
    scale_ref[...] = high[rest : rest + 1, :]
    slab = jnp.concatenate([low, high[:rest, :]], axis=0).astype(BF16)
    for i in range(copies):
        spread_ref[i] = slab


def expert_kernel(rows_ref, down_ref, gate_pre_ref, up_pre_ref, scale_ref, gate_ref, up_ref, term_ref):
    down_grad = dot(down_ref[...], rows_ref[...], (1, 0))
    gate_pre, up_pre = gate_pre_ref[...], up_pre_ref[...]
    sigmoid_gate = jax.nn.sigmoid(gate_pre)
    silu_value = gate_pre * sigmoid_gate
    score = jnp.sum(silu_value * up_pre * down_grad, axis=0, keepdims=True)
    hidden_grad = scale_ref[...] * down_grad
    gate_grad = hidden_grad * up_pre * sigmoid_gate * (1.0 + gate_pre * (1.0 - sigmoid_gate))
    up_grad = hidden_grad * silu_value
    grads = jnp.concatenate([gate_grad, up_grad], axis=0).astype(BF16)
    holders, padded, arrivals = term_ref.shape
    width = gate_ref.shape[1] // holders
    piece = 32
    for tile in range(gate_ref.shape[1] // LANES):
        at = slice(tile * LANES, (tile + 1) * LANES)
        weights = jnp.concatenate([gate_ref[:, at], up_ref[:, at]], axis=0)
        term = dot(weights, grads, (0, 0)).astype(BF16)
        for k in range(LANES // piece):
            first = tile * LANES + k * piece
            holder, offset = first // width, first % width
            term_ref[holder, offset : offset + piece, :] = term[k * piece : (k + 1) * piece]
    score_high = score.astype(BF16).astype(F32)
    extra_row = iota((padded - width, arrivals), 0)
    extra = jnp.where(extra_row == 0, score_high, jnp.where(extra_row == 1, score - score_high, 0.0))
    extra = extra.astype(BF16)
    for holder in range(holders):
        term_ref[holder, width:padded, :] = extra


def return_kernel(width, part_ref, back_ref):
    holders, padded, arrivals = part_ref.shape
    total = part_ref[0].astype(F32)
    for holder in range(1, holders):
        total = total + part_ref[holder].astype(F32)
    rows = back_ref.shape[0]
    score = total[width : width + 1, :] + total[width + 1 : width + 2, :]
    score_high = score.astype(BF16).astype(F32)
    extra_row = iota((2 * LANES - width, arrivals), 0)
    extra = jnp.where(extra_row == 0, score_high, jnp.where(extra_row == 1, score - score_high, 0.0))
    low = total[:LANES].astype(BF16)
    high = jnp.concatenate([total[LANES:width], extra], axis=0).astype(BF16)
    back = dot(pick(0, rows, arrivals), low, (1, 1)) + dot(pick(1, rows, arrivals), high, (1, 1))
    back_ref[...] = back.astype(BF16)


def combine_kernel(back_ref, place_ref, grad_ref, score_ref):
    tokens, width = grad_ref.shape
    rest = width - LANES
    back, place = back_ref[...], place_ref[...]
    sums = dot(place, back, (0, 0))
    low = sums[0:tokens]
    high = sums[GROUP_MOST * tokens : (GROUP_MOST + 1) * tokens]
    for i in range(1, GROUP_MOST):
        low = low + sums[i * tokens : (i + 1) * tokens]
        high = high + sums[(GROUP_MOST + i) * tokens : (GROUP_MOST + i + 1) * tokens]
    grad_ref[:, :LANES] = low.astype(BF16)
    grad_ref[:, LANES:] = high[:, :rest].astype(BF16)
    lane = iota((16, LANES), 1)
    chosen = (lane == rest + iota((16, LANES), 0)) & (iota((16, LANES), 0) < 2)
    scores = dot(chosen.astype(BF16), back, (1, 1)).astype(BF16)
    values = dot(scores, place, (1, 0))
    values = values[0:1] + values[1:2]
    for i in range(GROUP_MOST):
        first = (GROUP_MOST + i) * tokens
        score_ref[i : i + 1, :] = values[:, first : first + tokens]


def shape(dims, dtype):
    return jax.ShapeDtypeStruct(dims, dtype)


def on_device(out_grad, groups, route_weight, saved_input, w_gate, w_up, w_down):
    tokens, width = out_grad.shape
    nodes, holders = lax.axis_size("node"), lax.axis_size("local")
    rows, arrivals = nodes * 2 * CAP, nodes * CAP
    send, place = pl.pallas_call(
        send_kernel, out_shape=(shape((rows, LANES), BF16), shape((rows, LANES), BF16))
    )(out_grad, groups.T, route_weight.T)
    recv = lax.all_to_all(
        send.reshape(nodes, 2 * CAP, LANES), "node", split_axis=0, concat_axis=0, tiled=True
    ).reshape(rows, LANES)
    gate_pre = lax.dot_general(
        w_gate, saved_input, (((0,), (1,)), ((), ())), preferred_element_type=F32
    )
    up_pre = lax.dot_general(
        w_up, saved_input, (((0,), (1,)), ((), ())), preferred_element_type=F32
    )
    spread, scale = pl.pallas_call(
        spread_kernel, out_shape=(shape((holders, width, arrivals), BF16), shape((1, arrivals), F32))
    )(recv)
    full = lax.all_to_all(spread, "local", split_axis=0, concat_axis=0, tiled=True)
    term = pl.pallas_call(
        expert_kernel,
        out_shape=shape((holders, ROW_PAD, arrivals), BF16),
        compiler_params=pltpu.CompilerParams(vmem_limit_bytes=32 * 1024 * 1024),
    )(full.reshape(-1, arrivals), w_down, gate_pre, up_pre, scale, w_gate.T, w_up.T)
    part = lax.all_to_all(term, "local", split_axis=0, concat_axis=0, tiled=True)
    back = pl.pallas_call(
        lambda *refs: return_kernel(width, *refs), out_shape=shape((rows, LANES), BF16)
    )(part)
    back = lax.all_to_all(
        back.reshape(nodes, 2 * CAP, LANES), "node", split_axis=0, concat_axis=0, tiled=True
    ).reshape(rows, LANES)
    in_grad, score = pl.pallas_call(
        combine_kernel, out_shape=(shape((tokens, width), BF16), shape((GROUP_MOST, tokens), F32))
    )(back, place)
    return in_grad, score.T


def solution(mesh):
    placed = (
        P("node", "local"),
        P("node", None),
        P("node", None),
        P("node", None),
        P(None, ("node", "local")),
        P(None, ("node", "local")),
        P(("node", "local"), None),
    )
    return jax.shard_map(
        on_device,
        mesh=mesh,
        in_specs=placed,
        out_specs=(P("node", "local"), P("node", None)),
        check_vma=False,
    )
```

time: 324 us -> 164 us (0.51)
  waiting for transfers between devices: 132 us -> 21.1 us
  starting transfers between devices: 49.5 us -> 7.36 us
  between operations: 14.3 us -> 0.71 us
  blocking collectives: 105 us -> 117 us
  Pallas kernels: 0 us -> 11.4 us
  matrix products: 9.73 us -> 2.76 us
  local copies, waits for them, and re-layouts: 9.24 us -> 2.38 us
  other arithmetic: 3.33 us -> 0 us
    all_to_all x1 -> x3, blocking collectives: 54.4 us -> 117 us  [the longest x1 54.6 us: on_device(): lax.all_to_all(send.reshape(nodes, 2 * CAP, LANES), 'node', split_axis=0,...]
    unnamed x3 -> x0, waiting for transfers between devices: 58 us -> none
    psum x1 -> x0, blocking collectives: 50.8 us -> none  [on_device(): score_send = lax.psum(own_score, 'local')]
    all_to_all x3 -> x1, starting transfers between devices: 49.4 us -> 7.36 us  [on_device(): lax.all_to_all(spread, 'local', split_axis=0, concat_axis=0, tiled=True)]
    all_gather x1 -> x0, waiting for transfers between devices: 31 us -> none  [on_device(): full_grad = lax.all_gather(slice_grad, 'local', axis=1, tiled=True)]
    all_to_all x3 -> x1, waiting for transfers between devices: 42.8 us -> 21.1 us  [on_device(): lax.all_to_all(spread, 'local', split_axis=0, concat_axis=0, tiled=True)]
    pallas_call x0 -> x5, Pallas kernels: none -> 11.4 us  [the longest x1 2.61 us: on_device(): pl.pallas_call(lambda *refs: return_kernel(width, *refs), out_shape=shape...]
    dot_general x9 -> x2, matrix products: 9.73 us -> 2.76 us  [the longest x1 2.01 us: on_device(): lax.dot_general(w_up, saved_input, (((0,), (1,)), ((), ())), preferred_el...]
  transfers between devices with their start and end apart: 5 -> 1, of which waited for: 4 -> 1; matrix products, arithmetic and copies ran while one was open for 3% -> 2% of each run, Pallas kernels for 0% -> 0%
where the time goes in v1:
time: 164 us; the launch traced here: 163 us
  blocking collectives  117 us (71%)
  waiting for transfers between devices  21.1 us (13%)
  Pallas kernels  11.4 us (7%)
  starting transfers between devices  7.36 us (4%)
  matrix products  2.76 us (2%)
  local copies, waits for them, and re-layouts  2.38 us (1%)
    all_to_all x1, blocking collectives, on_device(): lax.all_to_all(send.reshape(nodes, 2 * CAP, LANES), 'node', split_axis=0,...  54.6 us
    all_to_all x1, blocking collectives, on_device(): lax.all_to_all(back.reshape(nodes, 2 * CAP, LANES), 'node', split_axis=0,...  31.3 us
    all_to_all x1, blocking collectives, on_device(): lax.all_to_all(term, 'local', split_axis=0, concat_axis=0, tiled=True)  31.1 us
    all_to_all x1, waiting for transfers between devices, on_device(): lax.all_to_all(spread, 'local', split_axis=0, concat_axis=0, tiled=True)  21.1 us
    all_to_all x1, starting transfers between devices, on_device(): lax.all_to_all(spread, 'local', split_axis=0, concat_axis=0, tiled=True)  7.36 us
  transfers between devices with their start and end apart: 1, of which 1 were waited for; matrix products, arithmetic and copies ran while one was open for 2% of the time, Pallas kernels for 0%

profile of v1, /device:TPU:24, one launch (start us, length us, event | category | flops | bytes accessed | tf_op | source)
XLA Modules:
  0.0 162.6 jit_solution(11258816377204811358)
XLA Ops:
  0.6 0.0 copy-start
  0.6 2.1 %shard_map.86 = (bf16[256,128]{1,0:T(8,128)(2,1)}, bf16[256,128]{1,0:T(8,128)(2,1)}) custom-call(bf16[16,224]{1,0:T(8,128)(2,1)} %grad_ref.1, s32[4,16]{1,0:T(4,128)} %bitcast.20, f32[4,16]{1,0:T(4,128)} %bitcast.21), custom_call_target="tpu_custom_call" | custom-call | tf_op jit(solution)/shard_map/pallas_call | solution.py:150
  2.7 54.6 %all_to_all.20 = bf16[32,8,128]{2,1,0:T(8,128)(2,1)} all-to-all(bf16[32,8,128]{2,1,0:T(8,128)(2,1)} %bitcast.19), channel_id=1, replica_groups=mesh['node'=32,'local'=32] {'node'}, dimensions={0} | all-to-all | bytes 131072 | tf_op jit(solution)/shard_map/all_to_all | solution.py:153
  57.3 2.4 %shard_map.87 = (bf16[32,224,128]{2,1,0:T(8,128)(2,1)}, f32[1,128]{1,0:T(1,128)}) custom-call(bf16[256,128]{1,0:T(8,128)(2,1)} %bitcast.18), custom_call_target="tpu_custom_call" | custom-call | tf_op jit(solution)/shard_map/pallas_call | solution.py:162
  59.7 7.4 %all-to-all-start.1 = ((bf16[32,224,128]{2,1,0:T(8,128)(2,1)}), bf16[32,224,128]{2,1,0:T(8,128)(2,1)}, u32[]{:S(2)}, u32[]{:S(2)}) async-start(bf16[32,224,128]{2,1,0:T(8,128)(2,1)} %get-tuple-element.9), calls=%async_computation.1 | async-start | bytes 3670016 | tf_op jit(solution)/shard_map/all_to_all | solution.py:165
  67.1 0.0 copy-done
  67.1 0.0 copy-start.1
  67.1 2.0 %fusion.1.up_pre_ref = f32[64,128]{1,0:T(8,128)S(1)} fusion(bf16[7168,64]{0,1:T(8,128)(2,1)} %param.12, bf16[128,7168]{1,0:T(8,128)(2,1)S(1)} %copy-done), kind=kOutput, calls=%fused_computation.1 | convolution fusion | flops 117440512 | bytes 2785280 | tf_op jit(solution)/shard_map/dot_general | solution.py:159
  69.1 0.0 copy-done.1
  69.2 0.0 copy-start.4
  69.2 0.7 fusion.gate_pre_ref
  69.9 21.1 %all-to-all-done.1 = bf16[32,224,128]{2,1,0:T(8,128)(2,1)} async-done(((bf16[32,224,128]{2,1,0:T(8,128)(2,1)}), bf16[32,224,128]{2,1,0:T(8,128)(2,1)}, u32[]{:S(2)}, u32[]{:S(2)}) %all-to-all-start.1) | async-done | bytes 1835040 | tf_op jit(solution)/shard_map/all_to_all | solution.py:165
  91.0 0.0 copy-done.4
  91.0 0.0 copy-start.2
  91.0 1.2 copy-done.2
  92.2 0.0 copy-start.3
  92.2 1.2 copy-done.3
  93.4 2.6 %shard_map.88 = bf16[32,240,128]{2,1,0:T(8,128)(2,1)S(1)} custom-call(bf16[7168,128]{1,0:T(8,128)(2,1)} %bitcast.4.rows_ref, bf16[64,7168]{1,0:T(8,128)(2,1)S(1)} %copy-done.3, f32[64,128]{1,0:T(8,128)S(1)} %fusion.gate_pre_ref, f32[64,128]{1,0:T(8,128)S(1)} %fusion.1.up_pre_ref, f32[1,128]{1,0:T(1,128)S(1)} %copy-done.4, bf16[64,7168]{1,0:T(8,128)(2,1)S(1)} %bitcast.14, ...), custom_call_target="tpu_custom_call" | custom-call | tf_op jit(solution)/shard_map/pallas_call | solution.py:166
  95.9 31.1 %all_to_all.21.refs_0_ = bf16[32,240,128]{2,1,0:T(8,128)(2,1)} all-to-all(bf16[32,240,128]{2,1,0:T(8,128)(2,1)S(1)} %shard_map.88), channel_id=1, replica_groups=mesh['node'=32,'local'=32] {'local'}, dimensions={0} | all-to-all | bytes 3932160 | tf_op jit(solution)/shard_map/all_to_all | solution.py:171
  127.0 2.6 %shard_map.89 = bf16[256,128]{1,0:T(8,128)(2,1)} custom-call(bf16[32,240,128]{2,1,0:T(8,128)(2,1)} %all_to_all.21.refs_0_), custom_call_target="tpu_custom_call" | custom-call | tf_op jit(solution)/shard_map/pallas_call | solution.py:172
  129.6 31.3 %all_to_all.22 = bf16[32,8,128]{2,1,0:T(8,128)(2,1)} all-to-all(bf16[32,8,128]{2,1,0:T(8,128)(2,1)} %bitcast.16), channel_id=1, replica_groups=mesh['node'=32,'local'=32] {'node'}, dimensions={0} | all-to-all | bytes 131072 | tf_op jit(solution)/shard_map/all_to_all | solution.py:175
  160.8 1.8 %shard_map.90 = (bf16[16,224]{1,0:T(8,128)(2,1)}, f32[4,16]{1,0:T(4,128)}) custom-call(bf16[256,128]{1,0:T(8,128)(2,1)} %bitcast.17, bf16[256,128]{1,0:T(8,128)(2,1)} %get-tuple-element.11.place_ref), custom_call_target="tpu_custom_call" | custom-call | tf_op jit(solution)/shard_map/pallas_call | solution.py:178
Async XLA Ops:
  0.6 66.5 %copy-start = (bf16[128,7168]{1,0:T(8,128)(2,1)S(1)}, bf16[128,7168]{1,0:T(8,128)(2,1)}, u32[]{:S(2)}) copy-start(bf16[128,7168]{1,0:T(8,128)(2,1)} %param.10) | copy-start | bytes 5505028
  59.7 31.3 %all-to-all-start.1 = ((bf16[32,224,128]{2,1,0:T(8,128)(2,1)}), bf16[32,224,128]{2,1,0:T(8,128)(2,1)}, u32[]{:S(2)}, u32[]{:S(2)}) async-start(bf16[32,224,128]{2,1,0:T(8,128)(2,1)} %get-tuple-element.9), calls=%async_computation.1 | async-start | bytes 3670016 | tf_op jit(solution)/shard_map/all_to_all | solution.py:165
  67.1 2.0 %copy-start.1 = (bf16[7168,64]{0,1:T(8,128)(2,1)S(1)}, bf16[7168,64]{0,1:T(8,128)(2,1)}, u32[]{:S(2)}) copy-start(bf16[7168,64]{0,1:T(8,128)(2,1)} %param.11) | copy-start | bytes 2752516
  69.2 21.8 %copy-start.4 = (f32[1,128]{1,0:T(1,128)S(1)}, f32[1,128]{1,0:T(1,128)}, u32[]{:S(2)}) copy-start(f32[1,128]{1,0:T(1,128)} %get-tuple-element.10.scale_ref) | copy-start | bytes 1540
  91.0 1.2 copy-start.2
  92.2 1.2 copy-start.3

commit v2 on v1

v2 whole, which is shorter than its diff:
```python
import jax
import jax.numpy as jnp
from jax import lax
from jax.experimental import pallas as pl
from jax.experimental.pallas import tpu as pltpu
from jax.sharding import PartitionSpec as P

GROUP_MOST = 4
CAP = 4
LANES = 128
BF16 = jnp.bfloat16
F32 = jnp.float32
ROW_PAD = 240


def dot(a, b, contract):
    return lax.dot_general(
        a, b, ((contract[:1], contract[1:]), ((), ())), preferred_element_type=F32
    )


def iota(shape, dim):
    return lax.broadcasted_iota(jnp.int32, shape, dim)


def chip_at(position, chips):
    return (position + 5 * chips // 8) % chips


def node_of(row, nodes):
    return (row // (2 * CAP) + nodes // 2) % nodes


def fetch(pairs, sems):
    copies = [pltpu.make_async_copy(src, dst, sems.at[i]) for i, (src, dst) in enumerate(pairs)]
    for copy in copies:
        copy.start()
    return copies


def placement(groups, rows):
    tokens = groups.shape[1]
    row = iota((tokens, rows), 1)
    node, half, slot = node_of(row, rows // (2 * CAP)), row // CAP % 2, row % CAP
    same = (iota((tokens, tokens), 0) == iota((tokens, tokens), 1)).astype(BF16)
    columns = dot(same, groups.astype(F32).astype(BF16), (1, 1)).astype(jnp.int32)
    named = [(columns[:, i : i + 1] == node).astype(F32) for i in range(GROUP_MOST)]
    visits = named[0] + named[1] + named[2] + named[3]
    earlier = (iota((tokens, tokens), 1) < iota((tokens, tokens), 0)).astype(BF16)
    rank = dot(earlier, visits.astype(BF16), (1, 0))
    here = (rank == slot.astype(F32)).astype(F32)
    return named, visits, here * (half == 0).astype(F32), here * (half == 1).astype(F32)


def send_kernel(grad_hbm, groups_hbm, weight_hbm, send_ref, grad_ref, groups_ref, weight_ref, sems):
    tokens, width = grad_ref.shape
    rows = send_ref.shape[0]
    rest = width - LANES
    copies = fetch(
        [(groups_hbm, groups_ref), (weight_hbm, weight_ref), (grad_hbm, grad_ref)], sems
    )
    copies[0].wait()
    named, visits, low, high = placement(groups_ref[...], rows)
    copies[1].wait()
    same = (iota((tokens, tokens), 0) == iota((tokens, tokens), 1)).astype(BF16)
    columns = dot(same, weight_ref[...].astype(BF16), (1, 1))
    scale = columns[:, 0:1] * named[0]
    for i in range(1, GROUP_MOST):
        scale = scale + columns[:, i : i + 1] * named[i]
    picks = jnp.concatenate([low * visits, high * visits, high * scale], axis=0).astype(BF16)
    copies[2].wait()
    grad = grad_ref[...].astype(F32)
    values = jnp.concatenate(
        [
            grad[:, :LANES],
            jnp.concatenate([grad[:, LANES:], jnp.zeros((tokens, LANES - rest), F32)], axis=1),
            (iota((tokens, LANES), 1) == rest).astype(F32),
        ],
        axis=0,
    ).astype(BF16)
    send_ref[...] = dot(picks, values, (0, 0)).astype(BF16)


def pick(half, rows, arrivals):
    row, arrival = iota((rows, arrivals), 0), iota((rows, arrivals), 1)
    same = (node_of(row, rows // (2 * CAP)) == arrival // CAP) & (row % CAP == arrival % CAP)
    return (same & (row // CAP % 2 == half)).astype(BF16)


def spread_kernel(recv_ref, spread_hbm, scale_ref, slab_ref, sems):
    rows = recv_ref.shape[0]
    width, arrivals = slab_ref.shape
    recv = recv_ref[...]
    low = dot(recv, pick(0, rows, arrivals), (0, 0))
    high = dot(recv, pick(1, rows, arrivals), (0, 0))
    rest = width - LANES
    scale_ref[...] = high[rest : rest + 1, :]
    slab_ref[...] = jnp.concatenate([low, high[:rest, :]], axis=0).astype(BF16)
    copies = fetch([(slab_ref, spread_hbm.at[i]) for i in range(spread_hbm.shape[0])], sems)
    for copy in copies:
        copy.wait()


def prepare_down_kernel(down_ref, down_pair_ref, prepared_ref, down_part_ref):
    units = down_ref.shape[0]
    chips, _, width = down_part_ref.shape
    core = lax.axis_index("core")
    for parity in range(2):

        @pl.when(core == parity)
        def _():
            for k in range(chips):
                first = (2 * chip_at(k, chips) + parity) * width
                down_part_ref[k, :units] = down_ref[:, first : first + width]
                down_part_ref[k, units:] = down_pair_ref[:, first : first + width]


def prepare_kernel(
    saved_hbm, gate_hbm, gate_pair_hbm, up_hbm, up_pair_hbm, groups_ref,
    pre_ref, back_part_ref, place_ref,
    saved_ref, weight_ref, sems,
):
    units = gate_hbm.shape[0]
    chips, width, _ = back_part_ref.shape
    copies = fetch(
        [
            (gate_hbm, weight_ref.at[pl.ds(0, units)]),
            (gate_pair_hbm, weight_ref.at[pl.ds(units, units)]),
            (up_hbm, weight_ref.at[pl.ds(2 * units, units)]),
            (up_pair_hbm, weight_ref.at[pl.ds(3 * units, units)]),
            (saved_hbm, saved_ref),
        ],
        sems,
    )
    named, _, low, high = placement(groups_ref[...], place_ref.shape[1])
    parts = [part * named[i] for part in (low, high) for i in range(GROUP_MOST)]
    place_ref[...] = jnp.concatenate(parts, axis=0).astype(BF16)
    core = lax.axis_index("core")
    for copy in copies[:4]:
        copy.wait()
    for parity in range(2):

        @pl.when(core == parity)
        def _():
            for k in range(chips):
                first = (2 * chip_at(k, chips) + parity) * width
                back_part_ref[k] = weight_ref[:, first : first + width].T

    copies[4].wait()
    pre_ref[...] = dot(weight_ref[...], saved_ref[...], (1, 1))


def down_kernel(rows_ref, down_ref, part_ref):
    total = dot(down_ref[0], rows_ref[0], (1, 0))
    for k in range(1, rows_ref.shape[0]):
        total = total + dot(down_ref[k], rows_ref[k], (1, 0))
    part_ref[...] = total


def expert_kernel(part_ref, pair_ref, pre_ref, scale_ref, weight_ref, term_ref):
    units = part_ref.shape[0] // 2
    pair = pair_ref[...]
    down_grad = part_ref[...] + jnp.concatenate([pair[units:], pair[:units]], axis=0)
    gate_pre, up_pre = pre_ref[: 2 * units, :], pre_ref[2 * units :, :]
    sigmoid_gate = jax.nn.sigmoid(gate_pre)
    silu_value = gate_pre * sigmoid_gate
    score = jnp.sum(silu_value * up_pre * down_grad, axis=0, keepdims=True)
    hidden_grad = scale_ref[...] * down_grad
    gate_grad = hidden_grad * up_pre * sigmoid_gate * (1.0 + gate_pre * (1.0 - sigmoid_gate))
    up_grad = hidden_grad * silu_value
    grads = jnp.concatenate([gate_grad, up_grad], axis=0).astype(BF16)
    chips, padded, arrivals = term_ref.shape
    width = weight_ref.shape[1]
    score_high = score.astype(BF16).astype(F32)
    extra_row = iota((padded - width, arrivals), 0)
    extra = jnp.where(extra_row == 0, score_high, jnp.where(extra_row == 1, score - score_high, 0.0))
    extra = extra.astype(BF16)
    for k in range(chips):
        term_ref[k, :width, :] = dot(weight_ref[k], grads, (1, 0)).astype(BF16)
        term_ref[k, width:padded, :] = extra


def return_kernel(width, part_ref, back_ref):
    holders, padded, arrivals = part_ref.shape
    total = part_ref[0].astype(F32)
    for holder in range(1, holders):
        total = total + part_ref[holder].astype(F32)
    rows = back_ref.shape[0]
    score = total[width : width + 1, :] + total[width + 1 : width + 2, :]
    score_high = score.astype(BF16).astype(F32)
    extra_row = iota((2 * LANES - width, arrivals), 0)
    extra = jnp.where(extra_row == 0, score_high, jnp.where(extra_row == 1, score - score_high, 0.0))
    low = total[:LANES].astype(BF16)
    high = jnp.concatenate([total[LANES:width], extra], axis=0).astype(BF16)
    back = dot(pick(0, rows, arrivals), low, (1, 1)) + dot(pick(1, rows, arrivals), high, (1, 1))
    back_ref[...] = back.astype(BF16)


def combine_kernel(back_ref, place_ref, grad_ref, score_ref):
    tokens, width = grad_ref.shape
    rest = width - LANES
    back, place = back_ref[...], place_ref[...]
    sums = dot(place, back, (1, 0))
    low = sums[0:tokens]
    high = sums[GROUP_MOST * tokens : (GROUP_MOST + 1) * tokens]
    for i in range(1, GROUP_MOST):
        low = low + sums[i * tokens : (i + 1) * tokens]
        high = high + sums[(GROUP_MOST + i) * tokens : (GROUP_MOST + i + 1) * tokens]
    grad_ref[:, :LANES] = low.astype(BF16)
    grad_ref[:, LANES:] = high[:, :rest].astype(BF16)
    lane = iota((16, LANES), 1)
    chosen = (lane == rest + iota((16, LANES), 0)) & (iota((16, LANES), 0) < 2)
    scores = dot(chosen.astype(BF16), back, (1, 1)).astype(BF16)
    values = dot(scores, place, (1, 1))
    values = values[0:1] + values[1:2]
    for i in range(GROUP_MOST):
        first = (GROUP_MOST + i) * tokens
        score_ref[i : i + 1, :] = values[:, first : first + tokens]


def shape(dims, dtype):
    return jax.ShapeDtypeStruct(dims, dtype)


def exchange(x, axis, groups=None):
    return lax.all_to_all(
        x, axis, split_axis=0, concat_axis=0, tiled=True, axis_index_groups=groups
    )


def memory(mebibytes):
    return pltpu.CompilerParams(vmem_limit_bytes=mebibytes * 1024 * 1024)


def swap(x):
    return lax.ppermute(x, "core", [(0, 1), (1, 0)])


def on_device(out_grad, groups, route_weight, saved_input, w_gate, w_up, w_down):
    tokens, width = out_grad.shape
    nodes, chips = lax.axis_size("node"), lax.axis_size("chip")
    rows, arrivals, units = nodes * 2 * CAP, nodes * CAP, w_down.shape[0]
    ring = [[(i + nodes // 2) % nodes for i in range(nodes)]]
    plane = [[chip_at(i, chips) for i in range(chips)]]
    hbm, vmem = pl.BlockSpec(memory_space=pltpu.HBM), pl.BlockSpec(memory_space=pltpu.VMEM)
    send = pl.pallas_call(
        send_kernel,
        in_specs=[hbm] * 3,
        out_shape=shape((rows, LANES), BF16),
        scratch_shapes=[
            pltpu.VMEM((tokens, width), BF16),
            pltpu.VMEM((GROUP_MOST, tokens), jnp.int32),
            pltpu.VMEM((GROUP_MOST, tokens), F32),
            pltpu.SemaphoreType.DMA((3,)),
        ],
    )(out_grad, groups.T, route_weight.T)
    w_gate, w_up = w_gate.T, w_up.T
    gate_pair, up_pair, down_pair = swap(w_gate), swap(w_up), swap(w_down)
    recv = exchange(send.reshape(nodes, 2 * CAP, LANES), "node", ring).reshape(rows, LANES)
    spread, scale = pl.pallas_call(
        spread_kernel,
        out_specs=(hbm, vmem),
        out_shape=(shape((chips, width, arrivals), BF16), shape((1, arrivals), F32)),
        scratch_shapes=[pltpu.VMEM((width, arrivals), BF16), pltpu.SemaphoreType.DMA((chips,))],
        compiler_params=memory(6),
    )(recv)
    features = saved_input.shape[1]
    pre, back_part, place = pl.pallas_call(
        prepare_kernel,
        in_specs=[hbm] * 5 + [vmem],
        out_shape=(
            shape((4 * units, arrivals), F32),
            shape((chips, width, 4 * units), BF16),
            shape((2 * GROUP_MOST * tokens, rows), BF16),
        ),
        scratch_shapes=[
            pltpu.VMEM((arrivals, features), BF16),
            pltpu.VMEM((4 * units, features), BF16),
            pltpu.SemaphoreType.DMA((5,)),
        ],
        compiler_params=memory(60),
        cost_estimate=pl.CostEstimate(
            flops=8 * units * arrivals * features, bytes_accessed=9 * 1024 * 1024, transcendentals=0
        ),
    )(saved_input, w_gate, gate_pair, w_up, up_pair, groups.T)
    down_part = pl.pallas_call(
        prepare_down_kernel,
        in_specs=[vmem, vmem, pl.BlockSpec(memory_space=pl.ANY)],
        out_shape=shape((chips, 2 * units, width), BF16),
        compiler_params=memory(6),
        cost_estimate=pl.CostEstimate(flops=0, bytes_accessed=4 * 1024 * 1024, transcendentals=0),
    )(w_down, down_pair, place)
    full = exchange(spread, "chip", plane)
    part = pl.pallas_call(
        down_kernel,
        out_shape=shape((2 * units, arrivals), F32),
        compiler_params=memory(6),
    )(full, down_part)
    pair = swap(part)
    term = pl.pallas_call(
        expert_kernel,
        out_shape=shape((chips, ROW_PAD, arrivals), BF16),
        compiler_params=memory(8),
    )(part, pair, pre, scale, back_part)
    terms = exchange(term, "chip", plane)
    back = pl.pallas_call(
        lambda *refs: return_kernel(width, *refs),
        out_shape=shape((rows, LANES), BF16),
        compiler_params=memory(6),
    )(terms)
    back = exchange(back.reshape(nodes, 2 * CAP, LANES), "node", ring).reshape(rows, LANES)
    in_grad, score = pl.pallas_call(
        combine_kernel,
        out_shape=(shape((tokens, width), BF16), shape((GROUP_MOST, tokens), F32)),
        compiler_params=memory(4),
    )(back, place)
    return in_grad, score.T


def solution(mesh):
    devices = mesh.devices
    split = jax.sharding.Mesh(
        devices.reshape(devices.shape[0], devices.shape[1] // 2, 2), ("node", "chip", "core")
    )
    local = ("chip", "core")
    every = ("node", "chip", "core")
    placed = (
        P("node", local),
        P("node", None),
        P("node", None),
        P("node", None),
        P(None, every),
        P(None, every),
        P(every, None),
    )
    return jax.shard_map(
        on_device,
        mesh=split,
        in_specs=placed,
        out_specs=(P("node", local), P("node", None)),
        check_vma=False,
    )
```

time: 164 us -> 121 us (0.74)
  blocking collectives: 117 us -> 46.3 us
  starting transfers between devices: 7.36 us -> 50.9 us
  waiting for transfers between devices: 21.1 us -> 7.02 us
  matrix products: 2.76 us -> 0 us
    all_to_all x3 -> x2, blocking collectives: 117 us -> 46.3 us  [exchange(): lax.all_to_all(x, axis, split_axis=0, concat_axis=0, tiled=True, axis_ind...]
    all_to_all x1 -> x2, starting transfers between devices: 7.36 us -> 42.6 us  [exchange(): lax.all_to_all(x, axis, split_axis=0, concat_axis=0, tiled=True, axis_ind...]
    all_to_all x1 -> x2, waiting for transfers between devices: 21.1 us -> 5.79 us  [exchange(): lax.all_to_all(x, axis, split_axis=0, concat_axis=0, tiled=True, axis_ind...]
    ppermute x0 -> x4, starting transfers between devices: none -> 8.31 us  [swap(): return lax.ppermute(x, 'core', [(0, 1), (1, 0)])]
    pallas_call x3 -> x6, Pallas kernels: 7.04 us -> 10.6 us  [the longest x1 5.86 us: on_device(): pl.pallas_call(prepare_kernel, in_specs=[hbm] * 5 + [vmem], out_shape=(sh...]
    dot_general x2 -> x0, matrix products: 2.76 us -> none  [the longest x1 2.01 us: on_device(): lax.dot_general(w_up, saved_input, (((0,), (1,)), ((), ())), preferred_el...]
    pallas_call x1, Pallas kernels: 2.61 us -> 0.32 us  [on_device(): pl.pallas_call(lambda *refs: return_kernel(width, *refs), out_shape=shape...]
  transfers between devices with their start and end apart: 1 -> 6, of which waited for: 1 -> 2; matrix products, arithmetic and copies ran while one was open for 2% -> 0% of each run, Pallas kernels for 0% -> 6%
where the time goes in v2:
time: 121 us; the launch traced here: 120 us
  starting transfers between devices  50.9 us (42%)
  blocking collectives  46.3 us (38%)
  Pallas kernels  11.9 us (10%)
  waiting for transfers between devices  7.02 us (6%)
  local copies, waits for them, and re-layouts  2.96 us (2%)
    all_to_all x2, blocking collectives, exchange(): lax.all_to_all(x, axis, split_axis=0, concat_axis=0, tiled=True, axis_ind...  46.3 us
    all_to_all x2, starting transfers between devices, exchange(): lax.all_to_all(x, axis, split_axis=0, concat_axis=0, tiled=True, axis_ind...  42.6 us
    ppermute x4, starting transfers between devices, swap(): return lax.ppermute(x, 'core', [(0, 1), (1, 0)])  8.31 us
    pallas_call x1, Pallas kernels, on_device(): pl.pallas_call(prepare_kernel, in_specs=[hbm] * 5 + [vmem], out_shape=(sh...  5.86 us
    all_to_all x2, waiting for transfers between devices, exchange(): lax.all_to_all(x, axis, split_axis=0, concat_axis=0, tiled=True, axis_ind...  5.79 us
    unnamed x14, local copies, waits for them, and re-layouts  2.96 us
  transfers between devices with their start and end apart: 6, of which 2 were waited for; matrix products, arithmetic and copies ran while one was open for 0% of the time, Pallas kernels for 6%

profile of v2, /device:TPU:24, one launch (start us, length us, event | category | flops | bytes accessed | tf_op | source)
XLA Modules:
  0.0 119.9 jit_solution(15404465114465110336)
XLA Ops:
  0.6 2.0 %shard_map.86 = bf16[256,128]{1,0:T(8,128)(2,1)} custom-call(bf16[16,224]{1,0:T(8,128)(2,1)} %grad_hbm.1, s32[4,16]{1,0:T(4,128)} %bitcast.17, f32[4,16]{1,0:T(4,128)} %bitcast.19), custom_call_target="tpu_custom_call" | custom-call | tf_op jit(solution)/shard_map/pallas_call | solution.py:246
  2.7 35.9 %all-to-all-start = ((bf16[32,8,128]{2,1,0:T(8,128)(2,1)}), bf16[32,8,128]{2,1,0:T(8,128)(2,1)S(1)}, u32[]{:S(2)}, u32[]{:S(2)}) async-start(bf16[32,8,128]{2,1,0:T(8,128)(2,1)} %bitcast.16), calls=%async_computation | async-start | bytes 131072 | tf_op jit(solution)/shard_map/all_to_all | solution.py:226
  38.6 1.9 %collective-permute-start.1 = (bf16[64,7168]{1,0:T(8,128)(2,1)}, bf16[64,7168]{1,0:T(8,128)(2,1)}, u32[]{:S(2)}, u32[]{:S(2)}) collective-permute-start(bf16[64,7168]{1,0:T(8,128)(2,1)} %bitcast.12), channel_id=1, source_target_pairs={{0,1},{1,0},{2,3},{3,2},{4,5},{5,4},{6,7},{7,6},{8,9},{9,8},{10,11... | collective-permute-start | bytes 2752520 | tf_op jit(solution)/shard_map/ppermute | solution.py:236
  40.5 2.4 %collective-permute-start.2 = (bf16[64,7168]{1,0:T(8,128)(2,1)}, bf16[64,7168]{1,0:T(8,128)(2,1)}, u32[]{:S(2)}, u32[]{:S(2)}) collective-permute-start(bf16[64,7168]{1,0:T(8,128)(2,1)} %bitcast.14), channel_id=1, source_target_pairs={{0,1},{1,0},{2,3},{3,2},{4,5},{5,4},{6,7},{7,6},{8,9},{9,8},{10,11... | collective-permute-start | bytes 2752520 | tf_op jit(solution)/shard_map/ppermute | solution.py:236
  42.9 1.9 %collective-permute-start = (bf16[64,7168]{1,0:T(8,128)(2,1)}, bf16[64,7168]{1,0:T(8,128)(2,1)S(1)}, u32[]{:S(2)}, u32[]{:S(2)}) collective-permute-start(bf16[64,7168]{1,0:T(8,128)(2,1)} %down_ref.1), channel_id=1, source_target_pairs={{0,1},{1,0},{2,3},{3,2},{4,5},{5,4},{6,7},{7,6},{8,9},{9,8},{10,11... | collective-permute-start | bytes 2752520 | tf_op jit(solution)/shard_map/ppermute | solution.py:236
  44.9 0.0 all-to-all-done
  44.9 1.3 %shard_map.87 = (bf16[16,224,128]{2,1,0:T(8,128)(2,1)}, f32[1,128]{1,0:T(1,128)S(1)}) custom-call(bf16[256,128]{1,0:T(8,128)(2,1)S(1)} %bitcast.10), custom_call_target="tpu_custom_call" | custom-call | tf_op jit(solution)/shard_map/pallas_call | solution.py:260
  46.2 6.7 %all-to-all-start.1 = ((bf16[16,224,128]{2,1,0:T(8,128)(2,1)}), bf16[16,224,128]{2,1,0:T(8,128)(2,1)S(1)}, u32[]{:S(2)}, u32[]{:S(2)}) async-start(bf16[16,224,128]{2,1,0:T(8,128)(2,1)} %get-tuple-element.9), calls=%async_computation.1 | async-start | bytes 1835008 | tf_op jit(solution)/shard_map/all_to_all | solution.py:226
  52.9 0.0 copy-start.1
  52.9 0.0 collective-permute-done.1.gate_pair_hbm
  52.9 0.0 collective-permute-done.2.up_pair_hbm
  52.9 5.9 %shard_map.88 = (f32[256,128]{1,0:T(8,128)}, bf16[16,224,256]{2,1,0:T(8,128)(2,1)}, bf16[128,256]{1,0:T(8,128)(2,1)}) custom-call(bf16[128,7168]{1,0:T(8,128)(2,1)} %saved_hbm.1, bf16[64,7168]{1,0:T(8,128)(2,1)} %bitcast.13, bf16[64,7168]{1,0:T(8,128)(2,1)} %collective-permute-done.1.gate_pair_hbm, bf16[64,7168]{1,0:T(8,128)(2,1)} %bitcast.15, ...), custom_call_target="tpu_custom_call" | custom-call | flops 469762048 | bytes 9437184 | tf_op jit(solution)/shard_map/pallas_call | solution.py:268
  58.8 0.0 collective-permute-done.down_pair_ref
  58.8 0.0 copy-start.2
  58.8 0.9 copy-done.2
  59.7 0.0 copy-done.1
  59.7 1.2 copy-done.3
  60.9 0.8 copy-done.4
  61.8 0.3 shard_map.89.down_ref
  62.1 5.8 %all-to-all-done.1.rows_ref = bf16[16,224,128]{2,1,0:T(8,128)(2,1)S(1)} async-done(((bf16[16,224,128]{2,1,0:T(8,128)(2,1)}), bf16[16,224,128]{2,1,0:T(8,128)(2,1)S(1)}, u32[]{:S(2)}, u32[]{:S(2)}) %all-to-all-start.1) | async-done | bytes 917536 | tf_op jit(solution)/shard_map/all_to_all | solution.py:226
  67.9 0.4 shard_map.90.part_ref
  68.3 2.1 %collective-permute-start.3 = (f32[128,128]{1,0:T(8,128)S(1)}, f32[128,128]{1,0:T(8,128)S(1)}, u32[]{:S(2)}, u32[]{:S(2)}) collective-permute-start(f32[128,128]{1,0:T(8,128)S(1)} %shard_map.90.part_ref), channel_id=1, source_target_pairs={{0,1},{1,0},{2,3},{3,2},{4,5},{5,4},{6,7},{7,6},{8,9},{9,8},{10,11... | collective-permute-start | bytes 196616 | tf_op jit(solution)/shard_map/ppermute | solution.py:236
  70.4 1.2 %collective-permute-done.3.pair_ref = f32[128,128]{1,0:T(8,128)S(1)} collective-permute-done((f32[128,128]{1,0:T(8,128)S(1)}, f32[128,128]{1,0:T(8,128)S(1)}, u32[]{:S(2)}, u32[]{:S(2)}) %collective-permute-start.3) | collective-permute-done | bytes 65568 | tf_op jit(solution)/shard_map/ppermute | solution.py:236
  71.6 0.0 copy-done.6
  71.6 0.0 copy-done
  71.6 0.7 shard_map.91
  72.3 0.0 copy-start.5
  72.3 19.8 %all_to_all.20.refs_0_ = bf16[16,240,128]{2,1,0:T(8,128)(2,1)S(1)} all-to-all(bf16[16,240,128]{2,1,0:T(8,128)(2,1)S(1)} %shard_map.91), channel_id=1, replica_groups={{20,22,24,26,28,30,0,2,4,6,8,10,12,14,16,18},{21,23,25,27,29,31,1,3,5,7..., dimensions={0} | all-to-all | bytes 1966080 | tf_op jit(solution)/shard_map/all_to_all | solution.py:226
  92.1 0.3 shard_map.92
  92.4 26.5 %all_to_all.21 = bf16[32,8,128]{2,1,0:T(8,128)(2,1)S(1)} all-to-all(bf16[32,8,128]{2,1,0:T(8,128)(2,1)S(1)} %bitcast.9), channel_id=1, replica_groups={{512,544,576,608,640,672,704,736,768,800,832,864,896,928,960,992,0,32,6..., dimensions={0} | all-to-all | bytes 131072 | tf_op jit(solution)/shard_map/all_to_all | solution.py:226
  119.0 0.0 copy-done.5
  119.0 0.9 shard_map.93
  (4 shorter events, 0.0 us)
Async XLA Ops:
  2.7 42.2 %all-to-all-start = ((bf16[32,8,128]{2,1,0:T(8,128)(2,1)}), bf16[32,8,128]{2,1,0:T(8,128)(2,1)S(1)}, u32[]{:S(2)}, u32[]{:S(2)}) async-start(bf16[32,8,128]{2,1,0:T(8,128)(2,1)} %bitcast.16), calls=%async_computation | async-start | bytes 131072 | tf_op jit(solution)/shard_map/all_to_all | solution.py:226
  38.6 14.3 %collective-permute-start.1 = (bf16[64,7168]{1,0:T(8,128)(2,1)}, bf16[64,7168]{1,0:T(8,128)(2,1)}, u32[]{:S(2)}, u32[]{:S(2)}) collective-permute-start(bf16[64,7168]{1,0:T(8,128)(2,1)} %bitcast.12), channel_id=1, source_target_pairs={{0,1},{1,0},{2,3},{3,2},{4,5},{5,4},{6,7},{7,6},{8,9},{9,8},{10,11... | collective-permute-start | bytes 2752520 | tf_op jit(solution)/shard_map/ppermute | solution.py:236
  40.5 12.4 %collective-permute-start.2 = (bf16[64,7168]{1,0:T(8,128)(2,1)}, bf16[64,7168]{1,0:T(8,128)(2,1)}, u32[]{:S(2)}, u32[]{:S(2)}) collective-permute-start(bf16[64,7168]{1,0:T(8,128)(2,1)} %bitcast.14), channel_id=1, source_target_pairs={{0,1},{1,0},{2,3},{3,2},{4,5},{5,4},{6,7},{7,6},{8,9},{9,8},{10,11... | collective-permute-start | bytes 2752520 | tf_op jit(solution)/shard_map/ppermute | solution.py:236
  42.9 15.9 %collective-permute-start = (bf16[64,7168]{1,0:T(8,128)(2,1)}, bf16[64,7168]{1,0:T(8,128)(2,1)S(1)}, u32[]{:S(2)}, u32[]{:S(2)}) collective-permute-start(bf16[64,7168]{1,0:T(8,128)(2,1)} %down_ref.1), channel_id=1, source_target_pairs={{0,1},{1,0},{2,3},{3,2},{4,5},{5,4},{6,7},{7,6},{8,9},{9,8},{10,11... | collective-permute-start | bytes 2752520 | tf_op jit(solution)/shard_map/ppermute | solution.py:236
  46.2 21.7 %all-to-all-start.1 = ((bf16[16,224,128]{2,1,0:T(8,128)(2,1)}), bf16[16,224,128]{2,1,0:T(8,128)(2,1)S(1)}, u32[]{:S(2)}, u32[]{:S(2)}) async-start(bf16[16,224,128]{2,1,0:T(8,128)(2,1)} %get-tuple-element.9), calls=%async_computation.1 | async-start | bytes 1835008 | tf_op jit(solution)/shard_map/all_to_all | solution.py:226
  52.9 6.8 %copy-start.1 = (bf16[64,7168]{1,0:T(8,128)(2,1)S(1)}, bf16[64,7168]{1,0:T(8,128)(2,1)}, u32[]{:S(2)}) copy-start(bf16[64,7168]{1,0:T(8,128)(2,1)} %down_ref.1) | copy-start | bytes 2752516
  58.8 0.9 copy-start.2
  59.7 1.2 copy-start.3
  60.9 0.8 copy-start.4
  61.8 9.8 %copy-start.6 = (f32[256,128]{1,0:T(8,128)S(1)}, f32[256,128]{1,0:T(8,128)}, u32[]{:S(2)}) copy-start(f32[256,128]{1,0:T(8,128)} %get-tuple-element.11.pre_ref) | copy-start | bytes 393220
  67.9 3.7 %copy-start = (bf16[16,224,256]{2,1,0:T(8,128)(2,1)S(1)}, bf16[16,224,256]{2,1,0:T(8,128)(2,1)}, u32[]{:S(2)}) copy-start(bf16[16,224,256]{2,1,0:T(8,128)(2,1)} %get-tuple-element.13.weight_ref) | copy-start | bytes 5505028
  68.3 3.3 %collective-permute-start.3 = (f32[128,128]{1,0:T(8,128)S(1)}, f32[128,128]{1,0:T(8,128)S(1)}, u32[]{:S(2)}, u32[]{:S(2)}) collective-permute-start(f32[128,128]{1,0:T(8,128)S(1)} %shard_map.90.part_ref), channel_id=1, source_target_pairs={{0,1},{1,0},{2,3},{3,2},{4,5},{5,4},{6,7},{7,6},{8,9},{9,8},{10,11... | collective-permute-start | bytes 196616 | tf_op jit(solution)/shard_map/ppermute | solution.py:236
  72.3 46.7 %copy-start.5 = (bf16[128,256]{1,0:T(8,128)(2,1)S(1)}, bf16[128,256]{1,0:T(8,128)(2,1)}, u32[]{:S(2)}) copy-start(bf16[128,256]{1,0:T(8,128)(2,1)} %get-tuple-element.10.prepared_ref.place_ref) | copy-start | bytes 196612

commit v3 on v2

--- a/solution.py
+++ b/solution.py
@@ -6,6 +6,7 @@
 from jax.sharding import PartitionSpec as P
 
 GROUP_MOST = 4
+FIRST_OUT, FIRST_BACK = 20, 16
 CAP = 4
 LANES = 128
 BF16 = jnp.bfloat16
@@ -27,8 +28,8 @@
     return (position + 5 * chips // 8) % chips
 
 
-def node_of(row, nodes):
-    return (row // (2 * CAP) + nodes // 2) % nodes
+def node_at(position, nodes, first):
+    return (position + first * nodes // 32) % nodes
 
 
 def fetch(pairs, sems):
@@ -38,18 +39,21 @@
     return copies
 
 
-def placement(groups, rows):
-    tokens = groups.shape[1]
+def placement(tokens, rows, first):
     row = iota((tokens, rows), 1)
-    node, half, slot = node_of(row, rows // (2 * CAP)), row // CAP % 2, row % CAP
-    same = (iota((tokens, tokens), 0) == iota((tokens, tokens), 1)).astype(BF16)
-    columns = dot(same, groups.astype(F32).astype(BF16), (1, 1)).astype(jnp.int32)
-    named = [(columns[:, i : i + 1] == node).astype(F32) for i in range(GROUP_MOST)]
-    visits = named[0] + named[1] + named[2] + named[3]
+    nodes = rows // (2 * CAP)
+    node = node_at(row // (2 * CAP), nodes, first).astype(F32)
+    half, slot = row // CAP % 2, (row % CAP).astype(F32)
+    low, high = (half == 0).astype(F32), (half == 1).astype(F32)
     earlier = (iota((tokens, tokens), 1) < iota((tokens, tokens), 0)).astype(BF16)
-    rank = dot(earlier, visits.astype(BF16), (1, 0))
-    here = (rank == slot.astype(F32)).astype(F32)
-    return named, visits, here * (half == 0).astype(F32), here * (half == 1).astype(F32)
+
+    def of(columns):
+        named = [(columns[:, i : i + 1] == node).astype(F32) for i in range(GROUP_MOST)]
+        visits = named[0] + named[1] + named[2] + named[3]
+        here = (dot(earlier, visits.astype(BF16), (1, 0)) == slot).astype(F32)
+        return named, visits, here * low, here * high
+
+    return of
 
 
 def send_kernel(grad_hbm, groups_hbm, weight_hbm, send_ref, grad_ref, groups_ref, weight_ref, sems):
@@ -59,14 +63,17 @@
     copies = fetch(
         [(groups_hbm, groups_ref), (weight_hbm, weight_ref), (grad_hbm, grad_ref)], sems
     )
+    place = placement(tokens, rows, FIRST_OUT)
+    same = (iota((tokens, tokens), 0) == iota((tokens, tokens), 1)).astype(BF16)
+    marks = (iota((tokens, LANES), 1) == rest).astype(F32)
     copies[0].wait()
-    named, visits, low, high = placement(groups_ref[...], rows)
     copies[1].wait()
-    same = (iota((tokens, tokens), 0) == iota((tokens, tokens), 1)).astype(BF16)
-    columns = dot(same, weight_ref[...].astype(BF16), (1, 1))
-    scale = columns[:, 0:1] * named[0]
+    both = jnp.concatenate([groups_ref[...].astype(F32), weight_ref[...]], axis=0)
+    columns = dot(same, both.astype(BF16), (1, 1))
+    named, visits, low, high = place(columns)
+    scale = columns[:, GROUP_MOST : GROUP_MOST + 1] * named[0]
     for i in range(1, GROUP_MOST):
-        scale = scale + columns[:, i : i + 1] * named[i]
+        scale = scale + columns[:, GROUP_MOST + i : GROUP_MOST + i + 1] * named[i]
     picks = jnp.concatenate([low * visits, high * visits, high * scale], axis=0).astype(BF16)
     copies[2].wait()
     grad = grad_ref[...].astype(F32)
@@ -74,16 +81,17 @@
         [
             grad[:, :LANES],
             jnp.concatenate([grad[:, LANES:], jnp.zeros((tokens, LANES - rest), F32)], axis=1),
-            (iota((tokens, LANES), 1) == rest).astype(F32),
+            marks,
         ],
         axis=0,
     ).astype(BF16)
     send_ref[...] = dot(picks, values, (0, 0)).astype(BF16)
 
 
-def pick(half, rows, arrivals):
+def pick(half, rows, arrivals, first):
     row, arrival = iota((rows, arrivals), 0), iota((rows, arrivals), 1)
-    same = (node_of(row, rows // (2 * CAP)) == arrival // CAP) & (row % CAP == arrival % CAP)
+    node = node_at(row // (2 * CAP), rows // (2 * CAP), first)
+    same = (node == arrival // CAP) & (row % CAP == arrival % CAP)
     return (same & (row // CAP % 2 == half)).astype(BF16)
 
 
@@ -91,8 +99,8 @@
     rows = recv_ref.shape[0]
     width, arrivals = slab_ref.shape
     recv = recv_ref[...]
-    low = dot(recv, pick(0, rows, arrivals), (0, 0))
-    high = dot(recv, pick(1, rows, arrivals), (0, 0))
+    low = dot(recv, pick(0, rows, arrivals, FIRST_OUT), (0, 0))
+    high = dot(recv, pick(1, rows, arrivals, FIRST_OUT), (0, 0))
     rest = width - LANES
     scale_ref[...] = high[rest : rest + 1, :]
     slab_ref[...] = jnp.concatenate([low, high[:rest, :]], axis=0).astype(BF16)
@@ -132,7 +140,10 @@
         ],
         sems,
     )
-    named, _, low, high = placement(groups_ref[...], place_ref.shape[1])
+    tokens = groups_ref.shape[1]
+    same = (iota((tokens, tokens), 0) == iota((tokens, tokens), 1)).astype(BF16)
+    columns = dot(same, groups_ref[...].astype(F32).astype(BF16), (1, 1))
+    named, _, low, high = placement(tokens, place_ref.shape[1], FIRST_BACK)(columns)
     parts = [part * named[i] for part in (low, high) for i in range(GROUP_MOST)]
     place_ref[...] = jnp.concatenate(parts, axis=0).astype(BF16)
     core = lax.axis_index("core")
@@ -192,7 +203,8 @@
     extra = jnp.where(extra_row == 0, score_high, jnp.where(extra_row == 1, score - score_high, 0.0))
     low = total[:LANES].astype(BF16)
     high = jnp.concatenate([total[LANES:width], extra], axis=0).astype(BF16)
-    back = dot(pick(0, rows, arrivals), low, (1, 1)) + dot(pick(1, rows, arrivals), high, (1, 1))
+    back = dot(pick(0, rows, arrivals, FIRST_BACK), low, (1, 1))
+    back = back + dot(pick(1, rows, arrivals, FIRST_BACK), high, (1, 1))
     back_ref[...] = back.astype(BF16)
 
 
@@ -240,7 +252,8 @@
     tokens, width = out_grad.shape
     nodes, chips = lax.axis_size("node"), lax.axis_size("chip")
     rows, arrivals, units = nodes * 2 * CAP, nodes * CAP, w_down.shape[0]
-    ring = [[(i + nodes // 2) % nodes for i in range(nodes)]]
+    ring_out = [[node_at(i, nodes, FIRST_OUT) for i in range(nodes)]]
+    ring_back = [[node_at(i, nodes, FIRST_BACK) for i in range(nodes)]]
     plane = [[chip_at(i, chips) for i in range(chips)]]
     hbm, vmem = pl.BlockSpec(memory_space=pltpu.HBM), pl.BlockSpec(memory_space=pltpu.VMEM)
     send = pl.pallas_call(
@@ -256,7 +269,7 @@
     )(out_grad, groups.T, route_weight.T)
     w_gate, w_up = w_gate.T, w_up.T
     gate_pair, up_pair, down_pair = swap(w_gate), swap(w_up), swap(w_down)
-    recv = exchange(send.reshape(nodes, 2 * CAP, LANES), "node", ring).reshape(rows, LANES)
+    recv = exchange(send.reshape(nodes, 2 * CAP, LANES), "node", ring_out).reshape(rows, LANES)
     spread, scale = pl.pallas_call(
         spread_kernel,
         out_specs=(hbm, vmem),
@@ -308,7 +321,7 @@
         out_shape=shape((rows, LANES), BF16),
         compiler_params=memory(6),
     )(terms)
-    back = exchange(back.reshape(nodes, 2 * CAP, LANES), "node", ring).reshape(rows, LANES)
+    back = exchange(back.reshape(nodes, 2 * CAP, LANES), "node", ring_back).reshape(rows, LANES)
     in_grad, score = pl.pallas_call(
         combine_kernel,
         out_shape=(shape((tokens, width), BF16), shape((GROUP_MOST, tokens), F32)),

time: 121 us -> 121 us (level); the launches traced: 120 us -> 118 us
  starting transfers between devices: 50.9 us -> 46.1 us
  waiting for transfers between devices: 7.02 us -> 10 us
    all_to_all x2, starting transfers between devices: 42.6 us -> 37.8 us  [exchange(): lax.all_to_all(x, axis, split_axis=0, concat_axis=0, tiled=True, axis_ind...]
    all_to_all x2, waiting for transfers between devices: 5.79 us -> 8.78 us  [exchange(): lax.all_to_all(x, axis, split_axis=0, concat_axis=0, tiled=True, axis_ind...]
  transfers between devices with their start and end apart: 6 -> 6, of which waited for: 2 -> 3; matrix products, arithmetic and copies ran while one was open for 0% -> 0% of each run, Pallas kernels for 6% -> 6%
where the time goes in v3:
time: 121 us; the launch traced here: 118 us
  blocking collectives  46.9 us (39%)
  starting transfers between devices  46.1 us (38%)
  Pallas kernels  11.7 us (10%)
  waiting for transfers between devices  10 us (8%)
  local copies, waits for them, and re-layouts  2.96 us (2%)
    all_to_all x2, blocking collectives, exchange(): lax.all_to_all(x, axis, split_axis=0, concat_axis=0, tiled=True, axis_ind...  46.9 us
    all_to_all x2, starting transfers between devices, exchange(): lax.all_to_all(x, axis, split_axis=0, concat_axis=0, tiled=True, axis_ind...  37.8 us
    all_to_all x2, waiting for transfers between devices, exchange(): lax.all_to_all(x, axis, split_axis=0, concat_axis=0, tiled=True, axis_ind...  8.78 us
    ppermute x4, starting transfers between devices, swap(): return lax.ppermute(x, 'core', [(0, 1), (1, 0)])  8.31 us
    pallas_call x1, Pallas kernels, on_device(): pl.pallas_call(prepare_kernel, in_specs=[hbm] * 5 + [vmem], out_shape=(sh...  5.86 us
    unnamed x14, local copies, waits for them, and re-layouts  2.96 us
  transfers between devices with their start and end apart: 6, of which 3 were waited for; matrix products, arithmetic and copies ran while one was open for 0% of the time, Pallas kernels for 6%

profile of v3, /device:TPU:24, one launch (start us, length us, event | category | flops | bytes accessed | tf_op | source)
XLA Modules:
  0.0 118.4 jit_solution(1922856816372544093)
XLA Ops:
  0.6 1.9 %shard_map.86 = bf16[256,128]{1,0:T(8,128)(2,1)} custom-call(bf16[16,224]{1,0:T(8,128)(2,1)} %grad_hbm.1, s32[4,16]{1,0:T(4,128)} %bitcast.17, f32[4,16]{1,0:T(4,128)} %bitcast.19), custom_call_target="tpu_custom_call" | custom-call | tf_op jit(solution)/shard_map/pallas_call | solution.py:259
  2.5 31.1 %all-to-all-start = ((bf16[32,8,128]{2,1,0:T(8,128)(2,1)}), bf16[32,8,128]{2,1,0:T(8,128)(2,1)S(1)}, u32[]{:S(2)}, u32[]{:S(2)}) async-start(bf16[32,8,128]{2,1,0:T(8,128)(2,1)} %bitcast.16), calls=%async_computation | async-start | bytes 131072 | tf_op jit(solution)/shard_map/all_to_all | solution.py:238
  33.6 1.9 %collective-permute-start.1 = (bf16[64,7168]{1,0:T(8,128)(2,1)}, bf16[64,7168]{1,0:T(8,128)(2,1)}, u32[]{:S(2)}, u32[]{:S(2)}) collective-permute-start(bf16[64,7168]{1,0:T(8,128)(2,1)} %bitcast.12), channel_id=1, source_target_pairs={{0,1},{1,0},{2,3},{3,2},{4,5},{5,4},{6,7},{7,6},{8,9},{9,8},{10,11... | collective-permute-start | bytes 2752520 | tf_op jit(solution)/shard_map/ppermute | solution.py:248
  35.5 2.4 %collective-permute-start.2 = (bf16[64,7168]{1,0:T(8,128)(2,1)}, bf16[64,7168]{1,0:T(8,128)(2,1)}, u32[]{:S(2)}, u32[]{:S(2)}) collective-permute-start(bf16[64,7168]{1,0:T(8,128)(2,1)} %bitcast.14), channel_id=1, source_target_pairs={{0,1},{1,0},{2,3},{3,2},{4,5},{5,4},{6,7},{7,6},{8,9},{9,8},{10,11... | collective-permute-start | bytes 2752520 | tf_op jit(solution)/shard_map/ppermute | solution.py:248
  38.0 1.9 %collective-permute-start = (bf16[64,7168]{1,0:T(8,128)(2,1)}, bf16[64,7168]{1,0:T(8,128)(2,1)S(1)}, u32[]{:S(2)}, u32[]{:S(2)}) collective-permute-start(bf16[64,7168]{1,0:T(8,128)(2,1)} %down_ref.1), channel_id=1, source_target_pairs={{0,1},{1,0},{2,3},{3,2},{4,5},{5,4},{6,7},{7,6},{8,9},{9,8},{10,11... | collective-permute-start | bytes 2752520 | tf_op jit(solution)/shard_map/ppermute | solution.py:248
  39.9 4.8 %all-to-all-done = bf16[32,8,128]{2,1,0:T(8,128)(2,1)S(1)} async-done(((bf16[32,8,128]{2,1,0:T(8,128)(2,1)}), bf16[32,8,128]{2,1,0:T(8,128)(2,1)S(1)}, u32[]{:S(2)}, u32[]{:S(2)}) %all-to-all-start) | async-done | bytes 65568 | tf_op jit(solution)/shard_map/all_to_all | solution.py:238
  44.6 1.3 %shard_map.87 = (bf16[16,224,128]{2,1,0:T(8,128)(2,1)}, f32[1,128]{1,0:T(1,128)S(1)}) custom-call(bf16[256,128]{1,0:T(8,128)(2,1)S(1)} %bitcast.10), custom_call_target="tpu_custom_call" | custom-call | tf_op jit(solution)/shard_map/pallas_call | solution.py:273
  46.0 6.7 %all-to-all-start.1 = ((bf16[16,224,128]{2,1,0:T(8,128)(2,1)}), bf16[16,224,128]{2,1,0:T(8,128)(2,1)S(1)}, u32[]{:S(2)}, u32[]{:S(2)}) async-start(bf16[16,224,128]{2,1,0:T(8,128)(2,1)} %get-tuple-element.9), calls=%async_computation.1 | async-start | bytes 1835008 | tf_op jit(solution)/shard_map/all_to_all | solution.py:238
  52.7 0.0 copy-start.1
  52.7 0.0 collective-permute-done.1.gate_pair_hbm
  52.7 0.0 collective-permute-done.2.up_pair_hbm
  52.7 5.9 %shard_map.88 = (f32[256,128]{1,0:T(8,128)}, bf16[16,224,256]{2,1,0:T(8,128)(2,1)}, bf16[128,256]{1,0:T(8,128)(2,1)}) custom-call(bf16[128,7168]{1,0:T(8,128)(2,1)} %saved_hbm.1, bf16[64,7168]{1,0:T(8,128)(2,1)} %bitcast.13, bf16[64,7168]{1,0:T(8,128)(2,1)} %collective-permute-done.1.gate_pair_hbm, bf16[64,7168]{1,0:T(8,128)(2,1)} %bitcast.15, ...), custom_call_target="tpu_custom_call" | custom-call | flops 469762048 | bytes 9437184 | tf_op jit(solution)/shard_map/pallas_call | solution.py:281
  58.6 0.0 collective-permute-done.down_pair_ref
  58.6 0.0 copy-start.2
  58.6 0.9 copy-done.2
  59.5 0.0 copy-done.1
  59.5 1.2 copy-done.3
  60.7 0.8 copy-done.4
  61.5 0.3 shard_map.89.down_ref
  61.9 4.0 %all-to-all-done.1.rows_ref = bf16[16,224,128]{2,1,0:T(8,128)(2,1)S(1)} async-done(((bf16[16,224,128]{2,1,0:T(8,128)(2,1)}), bf16[16,224,128]{2,1,0:T(8,128)(2,1)S(1)}, u32[]{:S(2)}, u32[]{:S(2)}) %all-to-all-start.1) | async-done | bytes 917536 | tf_op jit(solution)/shard_map/all_to_all | solution.py:238
  65.9 0.4 shard_map.90.part_ref
  66.3 2.1 %collective-permute-start.3 = (f32[128,128]{1,0:T(8,128)S(1)}, f32[128,128]{1,0:T(8,128)S(1)}, u32[]{:S(2)}, u32[]{:S(2)}) collective-permute-start(f32[128,128]{1,0:T(8,128)S(1)} %shard_map.90.part_ref), channel_id=1, source_target_pairs={{0,1},{1,0},{2,3},{3,2},{4,5},{5,4},{6,7},{7,6},{8,9},{9,8},{10,11... | collective-permute-start | bytes 196616 | tf_op jit(solution)/shard_map/ppermute | solution.py:248
  68.4 1.2 %collective-permute-done.3.pair_ref = f32[128,128]{1,0:T(8,128)S(1)} collective-permute-done((f32[128,128]{1,0:T(8,128)S(1)}, f32[128,128]{1,0:T(8,128)S(1)}, u32[]{:S(2)}, u32[]{:S(2)}) %collective-permute-start.3) | collective-permute-done | bytes 65568 | tf_op jit(solution)/shard_map/ppermute | solution.py:248
  69.6 0.0 copy-done.6
  69.6 0.0 copy-done
  69.6 0.6 shard_map.91
  70.3 0.0 copy-start.5
  70.3 19.8 %all_to_all.20.refs_0_ = bf16[16,240,128]{2,1,0:T(8,128)(2,1)S(1)} all-to-all(bf16[16,240,128]{2,1,0:T(8,128)(2,1)S(1)} %shard_map.91), channel_id=1, replica_groups={{20,22,24,26,28,30,0,2,4,6,8,10,12,14,16,18},{21,23,25,27,29,31,1,3,5,7..., dimensions={0} | all-to-all | bytes 1966080 | tf_op jit(solution)/shard_map/all_to_all | solution.py:238
  90.1 0.3 shard_map.92
  90.4 27.0 %all_to_all.21 = bf16[32,8,128]{2,1,0:T(8,128)(2,1)S(1)} all-to-all(bf16[32,8,128]{2,1,0:T(8,128)(2,1)S(1)} %bitcast.9), channel_id=1, replica_groups={{512,544,576,608,640,672,704,736,768,800,832,864,896,928,960,992,0,32,6..., dimensions={0} | all-to-all | bytes 131072 | tf_op jit(solution)/shard_map/all_to_all | solution.py:238
  117.5 0.0 copy-done.5
  117.5 0.9 shard_map.93
  (4 shorter events, 0.0 us)
Async XLA Ops:
  2.5 42.1 %all-to-all-start = ((bf16[32,8,128]{2,1,0:T(8,128)(2,1)}), bf16[32,8,128]{2,1,0:T(8,128)(2,1)S(1)}, u32[]{:S(2)}, u32[]{:S(2)}) async-start(bf16[32,8,128]{2,1,0:T(8,128)(2,1)} %bitcast.16), calls=%async_computation | async-start | bytes 131072 | tf_op jit(solution)/shard_map/all_to_all | solution.py:238
  33.6 19.1 %collective-permute-start.1 = (bf16[64,7168]{1,0:T(8,128)(2,1)}, bf16[64,7168]{1,0:T(8,128)(2,1)}, u32[]{:S(2)}, u32[]{:S(2)}) collective-permute-start(bf16[64,7168]{1,0:T(8,128)(2,1)} %bitcast.12), channel_id=1, source_target_pairs={{0,1},{1,0},{2,3},{3,2},{4,5},{5,4},{6,7},{7,6},{8,9},{9,8},{10,11... | collective-permute-start | bytes 2752520 | tf_op jit(solution)/shard_map/ppermute | solution.py:248
  35.5 17.1 %collective-permute-start.2 = (bf16[64,7168]{1,0:T(8,128)(2,1)}, bf16[64,7168]{1,0:T(8,128)(2,1)}, u32[]{:S(2)}, u32[]{:S(2)}) collective-permute-start(bf16[64,7168]{1,0:T(8,128)(2,1)} %bitcast.14), channel_id=1, source_target_pairs={{0,1},{1,0},{2,3},{3,2},{4,5},{5,4},{6,7},{7,6},{8,9},{9,8},{10,11... | collective-permute-start | bytes 2752520 | tf_op jit(solution)/shard_map/ppermute | solution.py:248
  38.0 20.6 %collective-permute-start = (bf16[64,7168]{1,0:T(8,128)(2,1)}, bf16[64,7168]{1,0:T(8,128)(2,1)S(1)}, u32[]{:S(2)}, u32[]{:S(2)}) collective-permute-start(bf16[64,7168]{1,0:T(8,128)(2,1)} %down_ref.1), channel_id=1, source_target_pairs={{0,1},{1,0},{2,3},{3,2},{4,5},{5,4},{6,7},{7,6},{8,9},{9,8},{10,11... | collective-permute-start | bytes 2752520 | tf_op jit(solution)/shard_map/ppermute | solution.py:248
  46.0 19.9 %all-to-all-start.1 = ((bf16[16,224,128]{2,1,0:T(8,128)(2,1)}), bf16[16,224,128]{2,1,0:T(8,128)(2,1)S(1)}, u32[]{:S(2)}, u32[]{:S(2)}) async-start(bf16[16,224,128]{2,1,0:T(8,128)(2,1)} %get-tuple-element.9), calls=%async_computation.1 | async-start | bytes 1835008 | tf_op jit(solution)/shard_map/all_to_all | solution.py:238
  52.7 6.8 %copy-start.1 = (bf16[64,7168]{1,0:T(8,128)(2,1)S(1)}, bf16[64,7168]{1,0:T(8,128)(2,1)}, u32[]{:S(2)}) copy-start(bf16[64,7168]{1,0:T(8,128)(2,1)} %down_ref.1) | copy-start | bytes 2752516
  58.6 0.9 copy-start.2
  59.5 1.2 copy-start.3
  60.7 0.8 copy-start.4
  61.5 8.1 %copy-start.6 = (f32[256,128]{1,0:T(8,128)S(1)}, f32[256,128]{1,0:T(8,128)}, u32[]{:S(2)}) copy-start(f32[256,128]{1,0:T(8,128)} %get-tuple-element.11.pre_ref) | copy-start | bytes 393220
  65.9 3.7 %copy-start = (bf16[16,224,256]{2,1,0:T(8,128)(2,1)S(1)}, bf16[16,224,256]{2,1,0:T(8,128)(2,1)}, u32[]{:S(2)}) copy-start(bf16[16,224,256]{2,1,0:T(8,128)(2,1)} %get-tuple-element.13.weight_ref) | copy-start | bytes 5505028
  66.3 3.3 %collective-permute-start.3 = (f32[128,128]{1,0:T(8,128)S(1)}, f32[128,128]{1,0:T(8,128)S(1)}, u32[]{:S(2)}, u32[]{:S(2)}) collective-permute-start(f32[128,128]{1,0:T(8,128)S(1)} %shard_map.90.part_ref), channel_id=1, source_target_pairs={{0,1},{1,0},{2,3},{3,2},{4,5},{5,4},{6,7},{7,6},{8,9},{9,8},{10,11... | collective-permute-start | bytes 196616 | tf_op jit(solution)/shard_map/ppermute | solution.py:248
  70.3 47.2 %copy-start.5 = (bf16[128,256]{1,0:T(8,128)(2,1)S(1)}, bf16[128,256]{1,0:T(8,128)(2,1)}, u32[]{:S(2)}) copy-start(bf16[128,256]{1,0:T(8,128)(2,1)} %get-tuple-element.10.prepared_ref.place_ref) | copy-start | bytes 196612

commit v4 on v3

--- a/solution.py
+++ b/solution.py
@@ -6,7 +6,7 @@
 from jax.sharding import PartitionSpec as P
 
 GROUP_MOST = 4
-FIRST_OUT, FIRST_BACK = 20, 16
+FIRST_OUT, FIRST_BACK = 22, 17
 CAP = 4
 LANES = 128
 BF16 = jnp.bfloat16
@@ -25,7 +25,7 @@
 
 
 def chip_at(position, chips):
-    return (position + 5 * chips // 8) % chips
+    return (position + 7 * chips // 8) % chips
 
 
 def node_at(position, nodes, first):

time: 121 us -> 120 us (level); the launches traced: 118 us -> 119 us
  starting transfers between devices: 46.1 us -> 44 us
  waiting for transfers between devices: 10 us -> 11.9 us
    all_to_all x2, starting transfers between devices: 37.8 us -> 35.7 us  [exchange(): lax.all_to_all(x, axis, split_axis=0, concat_axis=0, tiled=True, axis_ind...]
    all_to_all x2, waiting for transfers between devices: 8.78 us -> 10.7 us  [exchange(): lax.all_to_all(x, axis, split_axis=0, concat_axis=0, tiled=True, axis_ind...]
where the time goes in v4:
time: 120 us; the launch traced here: 119 us
  blocking collectives  47.8 us (40%)
  starting transfers between devices  44 us (37%)
  waiting for transfers between devices  11.9 us (10%)
  Pallas kernels  11.7 us (10%)
  local copies, waits for them, and re-layouts  2.96 us (2%)
    all_to_all x2, blocking collectives, exchange(): lax.all_to_all(x, axis, split_axis=0, concat_axis=0, tiled=True, axis_ind...  47.8 us
    all_to_all x2, starting transfers between devices, exchange(): lax.all_to_all(x, axis, split_axis=0, concat_axis=0, tiled=True, axis_ind...  35.7 us
    all_to_all x2, waiting for transfers between devices, exchange(): lax.all_to_all(x, axis, split_axis=0, concat_axis=0, tiled=True, axis_ind...  10.7 us
    ppermute x4, starting transfers between devices, swap(): return lax.ppermute(x, 'core', [(0, 1), (1, 0)])  8.31 us
    pallas_call x1, Pallas kernels, on_device(): pl.pallas_call(prepare_kernel, in_specs=[hbm] * 5 + [vmem], out_shape=(sh...  5.86 us
    unnamed x14, local copies, waits for them, and re-layouts  2.96 us
  transfers between devices with their start and end apart: 6, of which 3 were waited for; matrix products, arithmetic and copies ran while one was open for 0% of the time, Pallas kernels for 6%

profile of v4, /device:TPU:24, one launch (start us, length us, event | category | flops | bytes accessed | tf_op | source)
XLA Modules:
  0.0 119.2 jit_solution(13384970510232829766)
XLA Ops:
  0.6 1.9 %shard_map.86 = bf16[256,128]{1,0:T(8,128)(2,1)} custom-call(bf16[16,224]{1,0:T(8,128)(2,1)} %grad_hbm.1, s32[4,16]{1,0:T(4,128)} %bitcast.17, f32[4,16]{1,0:T(4,128)} %bitcast.19), custom_call_target="tpu_custom_call" | custom-call | tf_op jit(solution)/shard_map/pallas_call | solution.py:259
  2.5 29.3 %all-to-all-start = ((bf16[32,8,128]{2,1,0:T(8,128)(2,1)}), bf16[32,8,128]{2,1,0:T(8,128)(2,1)S(1)}, u32[]{:S(2)}, u32[]{:S(2)}) async-start(bf16[32,8,128]{2,1,0:T(8,128)(2,1)} %bitcast.16), calls=%async_computation | async-start | bytes 131072 | tf_op jit(solution)/shard_map/all_to_all | solution.py:238
  31.8 1.9 %collective-permute-start.1 = (bf16[64,7168]{1,0:T(8,128)(2,1)}, bf16[64,7168]{1,0:T(8,128)(2,1)}, u32[]{:S(2)}, u32[]{:S(2)}) collective-permute-start(bf16[64,7168]{1,0:T(8,128)(2,1)} %bitcast.12), channel_id=1, source_target_pairs={{0,1},{1,0},{2,3},{3,2},{4,5},{5,4},{6,7},{7,6},{8,9},{9,8},{10,11... | collective-permute-start | bytes 2752520 | tf_op jit(solution)/shard_map/ppermute | solution.py:248
  33.7 2.4 %collective-permute-start.2 = (bf16[64,7168]{1,0:T(8,128)(2,1)}, bf16[64,7168]{1,0:T(8,128)(2,1)}, u32[]{:S(2)}, u32[]{:S(2)}) collective-permute-start(bf16[64,7168]{1,0:T(8,128)(2,1)} %bitcast.14), channel_id=1, source_target_pairs={{0,1},{1,0},{2,3},{3,2},{4,5},{5,4},{6,7},{7,6},{8,9},{9,8},{10,11... | collective-permute-start | bytes 2752520 | tf_op jit(solution)/shard_map/ppermute | solution.py:248
  36.2 1.9 %collective-permute-start = (bf16[64,7168]{1,0:T(8,128)(2,1)}, bf16[64,7168]{1,0:T(8,128)(2,1)S(1)}, u32[]{:S(2)}, u32[]{:S(2)}) collective-permute-start(bf16[64,7168]{1,0:T(8,128)(2,1)} %down_ref.1), channel_id=1, source_target_pairs={{0,1},{1,0},{2,3},{3,2},{4,5},{5,4},{6,7},{7,6},{8,9},{9,8},{10,11... | collective-permute-start | bytes 2752520 | tf_op jit(solution)/shard_map/ppermute | solution.py:248
  38.1 6.6 %all-to-all-done = bf16[32,8,128]{2,1,0:T(8,128)(2,1)S(1)} async-done(((bf16[32,8,128]{2,1,0:T(8,128)(2,1)}), bf16[32,8,128]{2,1,0:T(8,128)(2,1)S(1)}, u32[]{:S(2)}, u32[]{:S(2)}) %all-to-all-start) | async-done | bytes 65568 | tf_op jit(solution)/shard_map/all_to_all | solution.py:238
  44.7 1.3 %shard_map.87 = (bf16[16,224,128]{2,1,0:T(8,128)(2,1)}, f32[1,128]{1,0:T(1,128)S(1)}) custom-call(bf16[256,128]{1,0:T(8,128)(2,1)S(1)} %bitcast.10), custom_call_target="tpu_custom_call" | custom-call | tf_op jit(solution)/shard_map/pallas_call | solution.py:273
  46.1 6.4 %all-to-all-start.1 = ((bf16[16,224,128]{2,1,0:T(8,128)(2,1)}), bf16[16,224,128]{2,1,0:T(8,128)(2,1)S(1)}, u32[]{:S(2)}, u32[]{:S(2)}) async-start(bf16[16,224,128]{2,1,0:T(8,128)(2,1)} %get-tuple-element.9), calls=%async_computation.1 | async-start | bytes 1835008 | tf_op jit(solution)/shard_map/all_to_all | solution.py:238
  52.5 0.0 collective-permute-done.1.gate_pair_hbm
  52.5 0.0 collective-permute-done.2.up_pair_hbm
  52.5 5.9 %shard_map.88 = (f32[256,128]{1,0:T(8,128)}, bf16[16,224,256]{2,1,0:T(8,128)(2,1)}, bf16[128,256]{1,0:T(8,128)(2,1)}) custom-call(bf16[128,7168]{1,0:T(8,128)(2,1)} %saved_hbm.1, bf16[64,7168]{1,0:T(8,128)(2,1)} %bitcast.13, bf16[64,7168]{1,0:T(8,128)(2,1)} %collective-permute-done.1.gate_pair_hbm, bf16[64,7168]{1,0:T(8,128)(2,1)} %bitcast.15, ...), custom_call_target="tpu_custom_call" | custom-call | flops 469762048 | bytes 9437184 | tf_op jit(solution)/shard_map/pallas_call | solution.py:281
  58.4 0.0 collective-permute-done.down_pair_ref
  58.4 0.0 copy-start.2
  58.4 0.9 copy-done.2
  59.3 0.0 copy-done.1
  59.3 0.0 copy-start.3
  59.3 1.2 copy-done.3
  60.5 0.8 copy-done.4
  61.3 0.3 shard_map.89.down_ref
  61.7 4.1 %all-to-all-done.1.rows_ref = bf16[16,224,128]{2,1,0:T(8,128)(2,1)S(1)} async-done(((bf16[16,224,128]{2,1,0:T(8,128)(2,1)}), bf16[16,224,128]{2,1,0:T(8,128)(2,1)S(1)}, u32[]{:S(2)}, u32[]{:S(2)}) %all-to-all-start.1) | async-done | bytes 917536 | tf_op jit(solution)/shard_map/all_to_all | solution.py:238
  65.7 0.4 shard_map.90.part_ref
  66.2 2.1 %collective-permute-start.3 = (f32[128,128]{1,0:T(8,128)S(1)}, f32[128,128]{1,0:T(8,128)S(1)}, u32[]{:S(2)}, u32[]{:S(2)}) collective-permute-start(f32[128,128]{1,0:T(8,128)S(1)} %shard_map.90.part_ref), channel_id=1, source_target_pairs={{0,1},{1,0},{2,3},{3,2},{4,5},{5,4},{6,7},{7,6},{8,9},{9,8},{10,11... | collective-permute-start | bytes 196616 | tf_op jit(solution)/shard_map/ppermute | solution.py:248
  68.2 1.2 %collective-permute-done.3.pair_ref = f32[128,128]{1,0:T(8,128)S(1)} collective-permute-done((f32[128,128]{1,0:T(8,128)S(1)}, f32[128,128]{1,0:T(8,128)S(1)}, u32[]{:S(2)}, u32[]{:S(2)}) %collective-permute-start.3) | collective-permute-done | bytes 65568 | tf_op jit(solution)/shard_map/ppermute | solution.py:248
  69.5 0.0 copy-done.6
  69.5 0.0 copy-done
  69.5 0.6 shard_map.91
  70.1 0.0 copy-start.5
  70.1 20.6 %all_to_all.20.refs_0_ = bf16[16,240,128]{2,1,0:T(8,128)(2,1)S(1)} all-to-all(bf16[16,240,128]{2,1,0:T(8,128)(2,1)S(1)} %shard_map.91), channel_id=1, replica_groups={{28,30,0,2,4,6,8,10,12,14,16,18,20,22,24,26},{29,31,1,3,5,7,9,11,13,15,..., dimensions={0} | all-to-all | bytes 1966080 | tf_op jit(solution)/shard_map/all_to_all | solution.py:238
  90.7 0.3 shard_map.92
  91.0 27.2 %all_to_all.21 = bf16[32,8,128]{2,1,0:T(8,128)(2,1)S(1)} all-to-all(bf16[32,8,128]{2,1,0:T(8,128)(2,1)S(1)} %bitcast.9), channel_id=1, replica_groups={{544,576,608,640,672,704,736,768,800,832,864,896,928,960,992,0,32,64,96..., dimensions={0} | all-to-all | bytes 131072 | tf_op jit(solution)/shard_map/all_to_all | solution.py:238
  118.2 0.0 copy-done.5
  118.2 0.9 shard_map.93
  (4 shorter events, 0.0 us)
Async XLA Ops:
  2.5 42.2 %all-to-all-start = ((bf16[32,8,128]{2,1,0:T(8,128)(2,1)}), bf16[32,8,128]{2,1,0:T(8,128)(2,1)S(1)}, u32[]{:S(2)}, u32[]{:S(2)}) async-start(bf16[32,8,128]{2,1,0:T(8,128)(2,1)} %bitcast.16), calls=%async_computation | async-start | bytes 131072 | tf_op jit(solution)/shard_map/all_to_all | solution.py:238
  31.8 20.7 %collective-permute-start.1 = (bf16[64,7168]{1,0:T(8,128)(2,1)}, bf16[64,7168]{1,0:T(8,128)(2,1)}, u32[]{:S(2)}, u32[]{:S(2)}) collective-permute-start(bf16[64,7168]{1,0:T(8,128)(2,1)} %bitcast.12), channel_id=1, source_target_pairs={{0,1},{1,0},{2,3},{3,2},{4,5},{5,4},{6,7},{7,6},{8,9},{9,8},{10,11... | collective-permute-start | bytes 2752520 | tf_op jit(solution)/shard_map/ppermute | solution.py:248
  33.7 18.7 %collective-permute-start.2 = (bf16[64,7168]{1,0:T(8,128)(2,1)}, bf16[64,7168]{1,0:T(8,128)(2,1)}, u32[]{:S(2)}, u32[]{:S(2)}) collective-permute-start(bf16[64,7168]{1,0:T(8,128)(2,1)} %bitcast.14), channel_id=1, source_target_pairs={{0,1},{1,0},{2,3},{3,2},{4,5},{5,4},{6,7},{7,6},{8,9},{9,8},{10,11... | collective-permute-start | bytes 2752520 | tf_op jit(solution)/shard_map/ppermute | solution.py:248
  36.2 22.2 %collective-permute-start = (bf16[64,7168]{1,0:T(8,128)(2,1)}, bf16[64,7168]{1,0:T(8,128)(2,1)S(1)}, u32[]{:S(2)}, u32[]{:S(2)}) collective-permute-start(bf16[64,7168]{1,0:T(8,128)(2,1)} %down_ref.1), channel_id=1, source_target_pairs={{0,1},{1,0},{2,3},{3,2},{4,5},{5,4},{6,7},{7,6},{8,9},{9,8},{10,11... | collective-permute-start | bytes 2752520 | tf_op jit(solution)/shard_map/ppermute | solution.py:248
  46.1 19.7 %all-to-all-start.1 = ((bf16[16,224,128]{2,1,0:T(8,128)(2,1)}), bf16[16,224,128]{2,1,0:T(8,128)(2,1)S(1)}, u32[]{:S(2)}, u32[]{:S(2)}) async-start(bf16[16,224,128]{2,1,0:T(8,128)(2,1)} %get-tuple-element.9), calls=%async_computation.1 | async-start | bytes 1835008 | tf_op jit(solution)/shard_map/all_to_all | solution.py:238
  52.5 6.8 %copy-start.1 = (bf16[64,7168]{1,0:T(8,128)(2,1)S(1)}, bf16[64,7168]{1,0:T(8,128)(2,1)}, u32[]{:S(2)}) copy-start(bf16[64,7168]{1,0:T(8,128)(2,1)} %down_ref.1) | copy-start | bytes 2752516
  58.4 0.9 copy-start.2
  59.3 1.2 copy-start.3
  60.5 0.8 copy-start.4
  61.3 8.1 %copy-start.6 = (f32[256,128]{1,0:T(8,128)S(1)}, f32[256,128]{1,0:T(8,128)}, u32[]{:S(2)}) copy-start(f32[256,128]{1,0:T(8,128)} %get-tuple-element.11.pre_ref) | copy-start | bytes 393220
  65.7 3.7 %copy-start = (bf16[16,224,256]{2,1,0:T(8,128)(2,1)S(1)}, bf16[16,224,256]{2,1,0:T(8,128)(2,1)}, u32[]{:S(2)}) copy-start(bf16[16,224,256]{2,1,0:T(8,128)(2,1)} %get-tuple-element.13.weight_ref) | copy-start | bytes 5505028
  66.2 3.3 %collective-permute-start.3 = (f32[128,128]{1,0:T(8,128)S(1)}, f32[128,128]{1,0:T(8,128)S(1)}, u32[]{:S(2)}, u32[]{:S(2)}) collective-permute-start(f32[128,128]{1,0:T(8,128)S(1)} %shard_map.90.part_ref), channel_id=1, source_target_pairs={{0,1},{1,0},{2,3},{3,2},{4,5},{5,4},{6,7},{7,6},{8,9},{9,8},{10,11... | collective-permute-start | bytes 196616 | tf_op jit(solution)/shard_map/ppermute | solution.py:248
  70.1 48.1 %copy-start.5 = (bf16[128,256]{1,0:T(8,128)(2,1)S(1)}, bf16[128,256]{1,0:T(8,128)(2,1)}, u32[]{:S(2)}) copy-start(bf16[128,256]{1,0:T(8,128)(2,1)} %get-tuple-element.10.prepared_ref.place_ref) | copy-start | bytes 196612

commit v5 on v4

--- a/solution.py
+++ b/solution.py
@@ -99,12 +99,15 @@
     rows = recv_ref.shape[0]
     width, arrivals = slab_ref.shape
     recv = recv_ref[...]
-    low = dot(recv, pick(0, rows, arrivals, FIRST_OUT), (0, 0))
+    rest = width - LANES
+    chips = spread_hbm.shape[0]
+    slab_ref[:LANES, :] = dot(recv, pick(0, rows, arrivals, FIRST_OUT), (0, 0)).astype(BF16)
+    first, last = pl.ds(0, LANES), pl.ds(LANES, rest)
+    copies = fetch([(slab_ref.at[first], spread_hbm.at[i, first]) for i in range(chips)], sems.at[0])
     high = dot(recv, pick(1, rows, arrivals, FIRST_OUT), (0, 0))
-    rest = width - LANES
+    slab_ref[LANES:, :] = high[:rest, :].astype(BF16)
+    copies += fetch([(slab_ref.at[last], spread_hbm.at[i, last]) for i in range(chips)], sems.at[1])
     scale_ref[...] = high[rest : rest + 1, :]
-    slab_ref[...] = jnp.concatenate([low, high[:rest, :]], axis=0).astype(BF16)
-    copies = fetch([(slab_ref, spread_hbm.at[i]) for i in range(spread_hbm.shape[0])], sems)
     for copy in copies:
         copy.wait()
 
@@ -274,7 +277,7 @@
         spread_kernel,
         out_specs=(hbm, vmem),
         out_shape=(shape((chips, width, arrivals), BF16), shape((1, arrivals), F32)),
-        scratch_shapes=[pltpu.VMEM((width, arrivals), BF16), pltpu.SemaphoreType.DMA((chips,))],
+        scratch_shapes=[pltpu.VMEM((width, arrivals), BF16), pltpu.SemaphoreType.DMA((2, chips))],
         compiler_params=memory(6),
     )(recv)
     features = saved_input.shape[1]

time: 120 us -> 120 us (level)
  no operation moved by 1% of the time
where the time goes in v5:
time: 120 us; the launch traced here: 119 us
  blocking collectives  47.8 us (40%)
  starting transfers between devices  44 us (37%)
  Pallas kernels  11.9 us (10%)
  waiting for transfers between devices  11.9 us (10%)
  local copies, waits for them, and re-layouts  2.96 us (2%)
    all_to_all x2, blocking collectives, exchange(): lax.all_to_all(x, axis, split_axis=0, concat_axis=0, tiled=True, axis_ind...  47.8 us
    all_to_all x2, starting transfers between devices, exchange(): lax.all_to_all(x, axis, split_axis=0, concat_axis=0, tiled=True, axis_ind...  35.7 us
    all_to_all x2, waiting for transfers between devices, exchange(): lax.all_to_all(x, axis, split_axis=0, concat_axis=0, tiled=True, axis_ind...  10.7 us
    ppermute x4, starting transfers between devices, swap(): return lax.ppermute(x, 'core', [(0, 1), (1, 0)])  8.31 us
    pallas_call x1, Pallas kernels, on_device(): pl.pallas_call(prepare_kernel, in_specs=[hbm] * 5 + [vmem], out_shape=(sh...  5.86 us
    unnamed x14, local copies, waits for them, and re-layouts  2.96 us
  transfers between devices with their start and end apart: 6, of which 3 were waited for; matrix products, arithmetic and copies ran while one was open for 0% of the time, Pallas kernels for 6%

profile of v5, /device:TPU:24, one launch (start us, length us, event | category | flops | bytes accessed | tf_op | source)
XLA Modules:
  0.0 119.3 jit_solution(17760197793993893379)
XLA Ops:
  0.6 1.9 %shard_map.86 = bf16[256,128]{1,0:T(8,128)(2,1)} custom-call(bf16[16,224]{1,0:T(8,128)(2,1)} %grad_hbm.1, s32[4,16]{1,0:T(4,128)} %bitcast.17, f32[4,16]{1,0:T(4,128)} %bitcast.19), custom_call_target="tpu_custom_call" | custom-call | tf_op jit(solution)/shard_map/pallas_call | solution.py:262
  2.5 29.3 %all-to-all-start = ((bf16[32,8,128]{2,1,0:T(8,128)(2,1)}), bf16[32,8,128]{2,1,0:T(8,128)(2,1)S(1)}, u32[]{:S(2)}, u32[]{:S(2)}) async-start(bf16[32,8,128]{2,1,0:T(8,128)(2,1)} %bitcast.16), calls=%async_computation | async-start | bytes 131072 | tf_op jit(solution)/shard_map/all_to_all | solution.py:241
  31.8 1.9 %collective-permute-start.1 = (bf16[64,7168]{1,0:T(8,128)(2,1)}, bf16[64,7168]{1,0:T(8,128)(2,1)}, u32[]{:S(2)}, u32[]{:S(2)}) collective-permute-start(bf16[64,7168]{1,0:T(8,128)(2,1)} %bitcast.12), channel_id=1, source_target_pairs={{0,1},{1,0},{2,3},{3,2},{4,5},{5,4},{6,7},{7,6},{8,9},{9,8},{10,11... | collective-permute-start | bytes 2752520 | tf_op jit(solution)/shard_map/ppermute | solution.py:251
  33.7 2.4 %collective-permute-start.2 = (bf16[64,7168]{1,0:T(8,128)(2,1)}, bf16[64,7168]{1,0:T(8,128)(2,1)}, u32[]{:S(2)}, u32[]{:S(2)}) collective-permute-start(bf16[64,7168]{1,0:T(8,128)(2,1)} %bitcast.14), channel_id=1, source_target_pairs={{0,1},{1,0},{2,3},{3,2},{4,5},{5,4},{6,7},{7,6},{8,9},{9,8},{10,11... | collective-permute-start | bytes 2752520 | tf_op jit(solution)/shard_map/ppermute | solution.py:251
  36.2 1.9 %collective-permute-start = (bf16[64,7168]{1,0:T(8,128)(2,1)}, bf16[64,7168]{1,0:T(8,128)(2,1)S(1)}, u32[]{:S(2)}, u32[]{:S(2)}) collective-permute-start(bf16[64,7168]{1,0:T(8,128)(2,1)} %down_ref.1), channel_id=1, source_target_pairs={{0,1},{1,0},{2,3},{3,2},{4,5},{5,4},{6,7},{7,6},{8,9},{9,8},{10,11... | collective-permute-start | bytes 2752520 | tf_op jit(solution)/shard_map/ppermute | solution.py:251
  38.1 6.6 %all-to-all-done = bf16[32,8,128]{2,1,0:T(8,128)(2,1)S(1)} async-done(((bf16[32,8,128]{2,1,0:T(8,128)(2,1)}), bf16[32,8,128]{2,1,0:T(8,128)(2,1)S(1)}, u32[]{:S(2)}, u32[]{:S(2)}) %all-to-all-start) | async-done | bytes 65568 | tf_op jit(solution)/shard_map/all_to_all | solution.py:241
  44.7 1.5 %shard_map.87 = (bf16[16,224,128]{2,1,0:T(8,128)(2,1)}, f32[1,128]{1,0:T(1,128)S(1)}) custom-call(bf16[256,128]{1,0:T(8,128)(2,1)S(1)} %bitcast.10), custom_call_target="tpu_custom_call" | custom-call | tf_op jit(solution)/shard_map/pallas_call | solution.py:276
  46.2 6.4 %all-to-all-start.1 = ((bf16[16,224,128]{2,1,0:T(8,128)(2,1)}), bf16[16,224,128]{2,1,0:T(8,128)(2,1)S(1)}, u32[]{:S(2)}, u32[]{:S(2)}) async-start(bf16[16,224,128]{2,1,0:T(8,128)(2,1)} %get-tuple-element.9), calls=%async_computation.1 | async-start | bytes 1835008 | tf_op jit(solution)/shard_map/all_to_all | solution.py:241
  52.6 0.0 copy-start.1
  52.6 0.0 collective-permute-done.1.gate_pair_hbm
  52.6 0.0 collective-permute-done.2.up_pair_hbm
  52.7 5.9 %shard_map.88 = (f32[256,128]{1,0:T(8,128)}, bf16[16,224,256]{2,1,0:T(8,128)(2,1)}, bf16[128,256]{1,0:T(8,128)(2,1)}) custom-call(bf16[128,7168]{1,0:T(8,128)(2,1)} %saved_hbm.1, bf16[64,7168]{1,0:T(8,128)(2,1)} %bitcast.13, bf16[64,7168]{1,0:T(8,128)(2,1)} %collective-permute-done.1.gate_pair_hbm, bf16[64,7168]{1,0:T(8,128)(2,1)} %bitcast.15, ...), custom_call_target="tpu_custom_call" | custom-call | flops 469762048 | bytes 9437184 | tf_op jit(solution)/shard_map/pallas_call | solution.py:284
  58.5 0.0 collective-permute-done.down_pair_ref
  58.5 0.0 copy-start.2
  58.5 0.9 copy-done.2
  59.5 0.0 copy-done.1
  59.5 1.2 copy-done.3
  60.6 0.8 copy-done.4
  61.5 0.3 shard_map.89.down_ref
  61.8 4.1 %all-to-all-done.1.rows_ref = bf16[16,224,128]{2,1,0:T(8,128)(2,1)S(1)} async-done(((bf16[16,224,128]{2,1,0:T(8,128)(2,1)}), bf16[16,224,128]{2,1,0:T(8,128)(2,1)S(1)}, u32[]{:S(2)}, u32[]{:S(2)}) %all-to-all-start.1) | async-done | bytes 917536 | tf_op jit(solution)/shard_map/all_to_all | solution.py:241
  65.9 0.4 shard_map.90.part_ref
  66.3 2.1 %collective-permute-start.3 = (f32[128,128]{1,0:T(8,128)S(1)}, f32[128,128]{1,0:T(8,128)S(1)}, u32[]{:S(2)}, u32[]{:S(2)}) collective-permute-start(f32[128,128]{1,0:T(8,128)S(1)} %shard_map.90.part_ref), channel_id=1, source_target_pairs={{0,1},{1,0},{2,3},{3,2},{4,5},{5,4},{6,7},{7,6},{8,9},{9,8},{10,11... | collective-permute-start | bytes 196616 | tf_op jit(solution)/shard_map/ppermute | solution.py:251
  68.4 1.2 %collective-permute-done.3.pair_ref = f32[128,128]{1,0:T(8,128)S(1)} collective-permute-done((f32[128,128]{1,0:T(8,128)S(1)}, f32[128,128]{1,0:T(8,128)S(1)}, u32[]{:S(2)}, u32[]{:S(2)}) %collective-permute-start.3) | collective-permute-done | bytes 65568 | tf_op jit(solution)/shard_map/ppermute | solution.py:251
  69.6 0.0 copy-done.6
  69.6 0.0 copy-done
  69.6 0.6 shard_map.91
  70.3 0.0 copy-start.5
  70.3 20.6 %all_to_all.20.refs_0_ = bf16[16,240,128]{2,1,0:T(8,128)(2,1)S(1)} all-to-all(bf16[16,240,128]{2,1,0:T(8,128)(2,1)S(1)} %shard_map.91), channel_id=1, replica_groups={{28,30,0,2,4,6,8,10,12,14,16,18,20,22,24,26},{29,31,1,3,5,7,9,11,13,15,..., dimensions={0} | all-to-all | bytes 1966080 | tf_op jit(solution)/shard_map/all_to_all | solution.py:241
  90.8 0.3 shard_map.92
  91.2 27.2 %all_to_all.21 = bf16[32,8,128]{2,1,0:T(8,128)(2,1)S(1)} all-to-all(bf16[32,8,128]{2,1,0:T(8,128)(2,1)S(1)} %bitcast.9), channel_id=1, replica_groups={{544,576,608,640,672,704,736,768,800,832,864,896,928,960,992,0,32,64,96..., dimensions={0} | all-to-all | bytes 131072 | tf_op jit(solution)/shard_map/all_to_all | solution.py:241
  118.4 0.0 copy-done.5
  118.4 0.9 shard_map.93
  (4 shorter events, 0.0 us)
Async XLA Ops:
  2.5 42.2 %all-to-all-start = ((bf16[32,8,128]{2,1,0:T(8,128)(2,1)}), bf16[32,8,128]{2,1,0:T(8,128)(2,1)S(1)}, u32[]{:S(2)}, u32[]{:S(2)}) async-start(bf16[32,8,128]{2,1,0:T(8,128)(2,1)} %bitcast.16), calls=%async_computation | async-start | bytes 131072 | tf_op jit(solution)/shard_map/all_to_all | solution.py:241
  31.8 20.8 %collective-permute-start.1 = (bf16[64,7168]{1,0:T(8,128)(2,1)}, bf16[64,7168]{1,0:T(8,128)(2,1)}, u32[]{:S(2)}, u32[]{:S(2)}) collective-permute-start(bf16[64,7168]{1,0:T(8,128)(2,1)} %bitcast.12), channel_id=1, source_target_pairs={{0,1},{1,0},{2,3},{3,2},{4,5},{5,4},{6,7},{7,6},{8,9},{9,8},{10,11... | collective-permute-start | bytes 2752520 | tf_op jit(solution)/shard_map/ppermute | solution.py:251
  33.7 18.9 %collective-permute-start.2 = (bf16[64,7168]{1,0:T(8,128)(2,1)}, bf16[64,7168]{1,0:T(8,128)(2,1)}, u32[]{:S(2)}, u32[]{:S(2)}) collective-permute-start(bf16[64,7168]{1,0:T(8,128)(2,1)} %bitcast.14), channel_id=1, source_target_pairs={{0,1},{1,0},{2,3},{3,2},{4,5},{5,4},{6,7},{7,6},{8,9},{9,8},{10,11... | collective-permute-start | bytes 2752520 | tf_op jit(solution)/shard_map/ppermute | solution.py:251
  36.2 22.4 %collective-permute-start = (bf16[64,7168]{1,0:T(8,128)(2,1)}, bf16[64,7168]{1,0:T(8,128)(2,1)S(1)}, u32[]{:S(2)}, u32[]{:S(2)}) collective-permute-start(bf16[64,7168]{1,0:T(8,128)(2,1)} %down_ref.1), channel_id=1, source_target_pairs={{0,1},{1,0},{2,3},{3,2},{4,5},{5,4},{6,7},{7,6},{8,9},{9,8},{10,11... | collective-permute-start | bytes 2752520 | tf_op jit(solution)/shard_map/ppermute | solution.py:251
  46.2 19.7 %all-to-all-start.1 = ((bf16[16,224,128]{2,1,0:T(8,128)(2,1)}), bf16[16,224,128]{2,1,0:T(8,128)(2,1)S(1)}, u32[]{:S(2)}, u32[]{:S(2)}) async-start(bf16[16,224,128]{2,1,0:T(8,128)(2,1)} %get-tuple-element.9), calls=%async_computation.1 | async-start | bytes 1835008 | tf_op jit(solution)/shard_map/all_to_all | solution.py:241
  52.6 6.8 %copy-start.1 = (bf16[64,7168]{1,0:T(8,128)(2,1)S(1)}, bf16[64,7168]{1,0:T(8,128)(2,1)}, u32[]{:S(2)}) copy-start(bf16[64,7168]{1,0:T(8,128)(2,1)} %down_ref.1) | copy-start | bytes 2752516
  58.5 0.9 copy-start.2
  59.5 1.2 copy-start.3
  60.6 0.8 copy-start.4
  61.5 8.1 %copy-start.6 = (f32[256,128]{1,0:T(8,128)S(1)}, f32[256,128]{1,0:T(8,128)}, u32[]{:S(2)}) copy-start(f32[256,128]{1,0:T(8,128)} %get-tuple-element.11.pre_ref) | copy-start | bytes 393220
  65.9 3.7 %copy-start = (bf16[16,224,256]{2,1,0:T(8,128)(2,1)S(1)}, bf16[16,224,256]{2,1,0:T(8,128)(2,1)}, u32[]{:S(2)}) copy-start(bf16[16,224,256]{2,1,0:T(8,128)(2,1)} %get-tuple-element.13.weight_ref) | copy-start | bytes 5505028
  66.3 3.3 %collective-permute-start.3 = (f32[128,128]{1,0:T(8,128)S(1)}, f32[128,128]{1,0:T(8,128)S(1)}, u32[]{:S(2)}, u32[]{:S(2)}) collective-permute-start(f32[128,128]{1,0:T(8,128)S(1)} %shard_map.90.part_ref), channel_id=1, source_target_pairs={{0,1},{1,0},{2,3},{3,2},{4,5},{5,4},{6,7},{7,6},{8,9},{9,8},{10,11... | collective-permute-start | bytes 196616 | tf_op jit(solution)/shard_map/ppermute | solution.py:251
  70.3 48.1 %copy-start.5 = (bf16[128,256]{1,0:T(8,128)(2,1)S(1)}, bf16[128,256]{1,0:T(8,128)(2,1)}, u32[]{:S(2)}) copy-start(bf16[128,256]{1,0:T(8,128)(2,1)} %get-tuple-element.10.prepared_ref.place_ref) | copy-start | bytes 196612
